TPU v7x, 256 devices: a whole 4x4x8 slice. The times are simulated.
256 devices in a mesh: grp: 4 (over y), ext: 64 (over z, x, core).
Axes of the slice: x: 4, y: 4, z: 8, core: 2. Of those that a mesh axis runs over, the one named last changes fastest.
Arguments:
- tiles: bfloat16 [4608, 49, 2048], P(('grp', 'ext')), may hold values from -6 to 6
- tissue_index: int32 [256, 18], P(('grp', 'ext')), may hold values from 0 to 17, each once within a row
- tissue_count: int32 [256], P(('grp', 'ext')), may hold values from 0 to 16, as said below
- w_reduce: bfloat16 [2048, 512], replicated, may hold values from -0.125 to 0.125
- scale_reduce: float32 [512], replicated, may hold values from 0.5 to 2
- bias_reduce: float32 [512], replicated, may hold values from -3 to 3
- w_spatial: bfloat16 [3, 3, 512, 512], replicated, may hold values from -0.09375 to 0.09375
- scale_spatial: float32 [512], replicated, may hold values from 0.5 to 2
- bias_spatial: float32 [512], replicated, may hold values from -3 to 3
- w_expand: bfloat16 [512, 2048], replicated, may hold values from -0.25 to 0.25
- scale_expand: float32 [2048], replicated, may hold values from 0.5 to 2
- bias_expand: float32 [2048], replicated, may hold values from -3 to 3
Outputs:
- embeddings: bfloat16 [2048, 2048], P(('grp', 'ext'))
Inputs may be any that keep to these rules, and one draw needn't show every extreme that they name: Let S(d) be the sum of tissue_count over owners before owner d; then 8 * d <= S(d) <= 8 * (d + 1) for every d, and all counts sum to 2048.
All inputs are finite; a program needn't handle non-finite values.
Results may differ from a plain program's by a relative error of at most 0.0021.
Values may be sent and summed in bfloat16 or wider, within the bound.
A program may use at most 128 MiB of HBM per device.

v0:
```python
import jax
import jax.numpy as jnp
from jax import lax
from jax.sharding import Mesh
from jax.sharding import PartitionSpec as P

SIDE = 7
SEQ_DEV = 8
GRP_EXT = ("grp", "ext_0", "ext_1", "ext_2")


def laid_out(blocks, dim):
    lengths = list(blocks.shape[1:])
    lengths[dim] *= blocks.shape[0]
    return jnp.moveaxis(blocks, 0, dim).reshape(lengths)


def all_blocks(x, axes, order):
    blocks = x[None]
    for k in order:
        blocks = lax.all_gather(blocks, axes[k], axis=0, tiled=True)
    held = [lax.axis_size(axes[k]) for k in reversed(order)]
    blocks = blocks.reshape(*held, *x.shape)
    turned = sorted(range(len(order)), key=lambda place: order[len(order) - 1 - place])
    return blocks.transpose(*turned, *range(len(order), blocks.ndim)).reshape(-1, *x.shape)


def gathered_by_axis(x, axes, order, dim):
    return laid_out(all_blocks(x, axes, order), dim)


def passed_along(x, axis, by):
    devices = lax.axis_size(axis)
    pairs = [(i, i + by) for i in range(devices) if 0 <= i + by < devices]
    return lax.ppermute(x, axis, pairs)


def bottleneck(
    tile_maps,
    w_reduce,
    scale_reduce,
    bias_reduce,
    w_spatial,
    scale_spatial,
    bias_spatial,
    w_expand,
    scale_expand,
    bias_expand,
):
    count_tiles = tile_maps.shape[0]
    side_cells = SIDE
    channels = tile_maps.shape[2]
    inner = w_reduce.shape[1]
    flat_map = tile_maps.reshape(count_tiles * side_cells * side_cells, channels)
    reduced = jnp.maximum(
        jnp.dot(flat_map, w_reduce, preferred_element_type=jnp.float32) * scale_reduce
        + bias_reduce,
        0.0,
    ).astype(jnp.bfloat16)
    grid_map = reduced.reshape(count_tiles, side_cells, side_cells, inner)
    padded = jnp.pad(grid_map, ((0, 0), (1, 1), (1, 1), (0, 0)))
    summed = jnp.zeros((count_tiles * side_cells * side_cells, inner), jnp.float32)
    for row_shift in range(3):
        for col_shift in range(3):
            window = padded[
                :, row_shift : row_shift + side_cells, col_shift : col_shift + side_cells, :
            ].reshape(count_tiles * side_cells * side_cells, inner)
            summed = summed + jnp.dot(
                window, w_spatial[row_shift, col_shift], preferred_element_type=jnp.float32
            )
    spatial = jnp.maximum(summed * scale_spatial + bias_spatial, 0.0).astype(jnp.bfloat16)
    expanded = jnp.maximum(
        jnp.dot(spatial, w_expand, preferred_element_type=jnp.float32) * scale_expand
        + bias_expand
        + flat_map.astype(jnp.float32),
        0.0,
    )
    return jnp.mean(
        expanded.reshape(count_tiles, side_cells * side_cells, channels), axis=1
    ).astype(jnp.bfloat16)


def on_device(
    tiles,
    tissue_index,
    tissue_count,
    w_reduce,
    scale_reduce,
    bias_reduce,
    w_spatial,
    scale_spatial,
    bias_spatial,
    w_expand,
    scale_expand,
    bias_expand,
):
    shard_rows = SEQ_DEV
    owned_count = tissue_count[0]
    rank_here = lax.axis_index(GRP_EXT)
    every_count = gathered_by_axis(tissue_count, (("grp", "ext_0", "ext_1"), "ext_2"), (0, 1), 0)
    before = jnp.arange(every_count.shape[0], dtype=jnp.int32) < rank_here
    offset = jnp.sum(jnp.where(before, every_count, 0))
    backlog = offset - rank_here * shard_rows
    row_order = jnp.arange(shard_rows, dtype=jnp.int32)
    listing = tissue_index[0]
    last_slot = 2 * shard_rows - 1
    stay_slot = jnp.clip(row_order - backlog, 0, last_slot)
    spill_raw = shard_rows - backlog + row_order
    spill_live = spill_raw < owned_count
    spill_slot = jnp.clip(spill_raw, 0, last_slot)
    from_prior = row_order < backlog
    weights = (
        w_reduce,
        scale_reduce,
        bias_reduce,
        w_spatial,
        scale_spatial,
        bias_spatial,
        w_expand,
        scale_expand,
        bias_expand,
    )
    home_rows = bottleneck(tiles[listing[: 2 * shard_rows]], *weights)
    spill_rows = jnp.where(spill_live[:, None], home_rows[spill_slot], jnp.zeros((), jnp.bfloat16))
    arrived = passed_along(spill_rows, GRP_EXT, 1)
    return jnp.where(from_prior[:, None], arrived, home_rows[stay_slot])


def solution(mesh):
    torus = Mesh(
        mesh.devices.reshape(mesh.shape["grp"], 8, 4, 2), ("grp", "ext_0", "ext_1", "ext_2")
    )
    return jax.shard_map(
        on_device,
        mesh=torus,
        in_specs=(
            P(GRP_EXT, None, None),
            P(GRP_EXT, None),
            P(GRP_EXT),
            P(),
            P(),
            P(),
            P(),
            P(),
            P(),
            P(),
            P(),
            P(),
        ),
        out_specs=P(GRP_EXT, None),
        check_vma=False,
    )
```

profile of v0, /device:TPU:8, one launch (start us, length us, event | category | flops | bytes accessed | tf_op | source)
XLA Modules:
  0.0 129.2 jit_solution(13369131930683203362)
XLA Ops:
  0.0 0.0 copy-start
  0.0 0.8 fusion.29
  0.8 4.7 %gather_fusion = bf16[16,49,2048]{2,1,0:T(8,128)(2,1)} fusion(bf16[18,49,2048]{2,1,0:T(8,128)(2,1)} %param.12, s32[1024]{0:T(1024)S(1)} %pad_clamp_fusion.2), kind=kCustom, calls=%fused_computation | custom fusion | bytes 6422592 | tf_op jit(solution)/shard_map/gather | solution.py:123
  5.6 0.0 copy-start.7
  5.6 0.0 copy-start.8
  5.6 3.8 %reshape.135 = bf16[784,2048]{1,0:T(8,128)(2,1)} reshape(bf16[16,49,2048]{2,1,0:T(8,128)(2,1)} %gather_fusion) | data formatting | bytes 6422528 | tf_op jit(solution)/shard_map/reshape | solution.py:54
  9.4 0.0 copy-done.7
  9.4 0.0 copy-done.8
  9.4 4.4 %maximum_convert_fusion.1 = bf16[784,512]{1,0:T(8,128)(2,1)S(1)} fusion(bf16[784,2048]{1,0:T(8,128)(2,1)} %reshape.135, bf16[2048,512]{1,0:T(8,128)(2,1)} %param.15, f32[512]{0:T(512)S(1)} %copy-done.7, f32[512]{0:T(512)S(1)} %copy-done.8), kind=kOutput, calls=%fused_computation.13 | convolution fusion | flops 1645772800 | bytes 6115328 | tf_op jit(solution)/shard_map/dot_general | solution.py:56
  13.8 0.0 copy-start.1
  13.8 0.9 copy-done.1
  14.6 1.2 reshape.136
  15.9 6.3 %pad_slice_fusion = (bf16[16,7,7,512]{3,2,1,0:T(8,128)(2,1)S(1)}, bf16[16,7,7,512]{3,2,1,0:T(8,128)(2,1)}, bf16[16,7,7,512]{3,2,1,0:T(8,128)(2,1)}, bf16[16,7,7,...) fusion(bf16[16,7,7,512]{3,2,1,0:T(8,128)(2,1)} %reshape.136), kind=kLoop, calls=%fused_computation.4 | loop fusion | bytes 7225344 | tf_op jit(solution)/shard_map/slice | solution.py:65
  22.2 2.2 %reshape.140 = bf16[784,512]{1,0:T(8,128)(2,1)} reshape(bf16[16,7,7,512]{3,2,1,0:T(8,128)(2,1)} %get-tuple-element.8) | data formatting | bytes 1605632 | tf_op jit(solution)/shard_map/reshape | solution.py:67
  24.4 0.0 copy-start.2
  24.4 3.1 %fusion.8 = f32[784,512]{1,0:T(8,128)} fusion(bf16[784,512]{1,0:T(8,128)(2,1)} %copy-done.1, bf16[3,3,512,512]{3,2,1,0:T(8,128)(2,1)} %param.18), kind=kOutput, calls=%fused_computation.21 | convolution fusion | flops 411041792 | bytes 2932736 | tf_op jit(solution)/shard_map/dot_general | solution.py:68
  27.5 0.0 copy-done.2
  27.5 2.8 %fusion.10 = f32[784,512]{1,0:T(8,128)} fusion(bf16[784,512]{1,0:T(8,128)(2,1)S(1)} %copy-done.2, bf16[3,3,512,512]{3,2,1,0:T(8,128)(2,1)} %param.18), kind=kOutput, calls=%fused_computation.23 | convolution fusion | flops 411041792 | bytes 2932736 | tf_op jit(solution)/shard_map/dot_general | solution.py:68
  30.2 2.2 %reshape.139 = bf16[784,512]{1,0:T(8,128)(2,1)} reshape(bf16[16,7,7,512]{3,2,1,0:T(8,128)(2,1)} %get-tuple-element.7) | data formatting | bytes 1605632 | tf_op jit(solution)/shard_map/reshape | solution.py:67
  32.4 3.0 %fusion.12 = f32[784,512]{1,0:T(8,128)} fusion(bf16[784,512]{1,0:T(8,128)(2,1)} %reshape.139, bf16[3,3,512,512]{3,2,1,0:T(8,128)(2,1)} %param.18), kind=kOutput, calls=%fused_computation.25 | convolution fusion | flops 411041792 | bytes 2932736 | tf_op jit(solution)/shard_map/dot_general | solution.py:68
  35.4 2.1 %reshape.138 = bf16[784,512]{1,0:T(8,128)(2,1)} reshape(bf16[16,7,7,512]{3,2,1,0:T(8,128)(2,1)} %get-tuple-element.6) | data formatting | bytes 1605632 | tf_op jit(solution)/shard_map/reshape | solution.py:67
  37.6 3.0 %fusion.14 = f32[784,512]{1,0:T(8,128)} fusion(bf16[784,512]{1,0:T(8,128)(2,1)} %reshape.138, bf16[3,3,512,512]{3,2,1,0:T(8,128)(2,1)} %param.18), kind=kOutput, calls=%fused_computation.27 | convolution fusion | flops 411041792 | bytes 2932736 | tf_op jit(solution)/shard_map/dot_general | solution.py:68
  40.6 2.1 %reshape.137 = bf16[784,512]{1,0:T(8,128)(2,1)} reshape(bf16[16,7,7,512]{3,2,1,0:T(8,128)(2,1)} %get-tuple-element.12) | data formatting | bytes 1605632 | tf_op jit(solution)/shard_map/reshape | solution.py:67
  42.7 3.0 %fusion.16 = f32[784,512]{1,0:T(8,128)} fusion(bf16[784,512]{1,0:T(8,128)(2,1)} %reshape.137, bf16[3,3,512,512]{3,2,1,0:T(8,128)(2,1)} %param.18), kind=kOutput, calls=%fused_computation.29 | convolution fusion | flops 411041792 | bytes 2932736 | tf_op jit(solution)/shard_map/dot_general | solution.py:68
  45.8 2.1 %reshape.143 = bf16[784,512]{1,0:T(8,128)(2,1)} reshape(bf16[16,7,7,512]{3,2,1,0:T(8,128)(2,1)} %get-tuple-element.11) | data formatting | bytes 1605632 | tf_op jit(solution)/shard_map/reshape | solution.py:67
  47.9 3.0 %fusion.2 = f32[784,512]{1,0:T(8,128)} fusion(bf16[784,512]{1,0:T(8,128)(2,1)} %reshape.143, bf16[3,3,512,512]{3,2,1,0:T(8,128)(2,1)} %param.18), kind=kOutput, calls=%fused_computation.15 | convolution fusion | flops 411041792 | bytes 2932736 | tf_op jit(solution)/shard_map/dot_general | solution.py:68
  50.9 2.2 %reshape.142 = bf16[784,512]{1,0:T(8,128)(2,1)} reshape(bf16[16,7,7,512]{3,2,1,0:T(8,128)(2,1)} %get-tuple-element.10) | data formatting | bytes 1605632 | tf_op jit(solution)/shard_map/reshape | solution.py:67
  53.1 3.0 %fusion.4 = f32[784,512]{1,0:T(8,128)} fusion(bf16[784,512]{1,0:T(8,128)(2,1)} %reshape.142, bf16[3,3,512,512]{3,2,1,0:T(8,128)(2,1)} %param.18), kind=kOutput, calls=%fused_computation.17 | convolution fusion | flops 411041792 | bytes 2932736 | tf_op jit(solution)/shard_map/dot_general | solution.py:68
  56.2 2.2 %reshape.141 = bf16[784,512]{1,0:T(8,128)(2,1)} reshape(bf16[16,7,7,512]{3,2,1,0:T(8,128)(2,1)} %get-tuple-element.9) | data formatting | bytes 1605632 | tf_op jit(solution)/shard_map/reshape | solution.py:67
  58.4 0.0 copy-start.3
  58.4 0.0 copy-start.4
  58.4 0.0 copy-start.5
  58.4 0.0 copy-start.6
  58.4 3.1 %fusion.6 = f32[784,512]{1,0:T(8,128)} fusion(bf16[784,512]{1,0:T(8,128)(2,1)} %reshape.141, bf16[3,3,512,512]{3,2,1,0:T(8,128)(2,1)} %param.18), kind=kOutput, calls=%fused_computation.19 | convolution fusion | flops 411041792 | bytes 2932736 | tf_op jit(solution)/shard_map/dot_general | solution.py:68
  61.5 1.2 reshape.144
  62.7 0.0 copy-done
  62.7 0.0 copy-done.3
  62.7 0.0 copy-done.4
  62.7 0.0 copy-done.5
  62.7 0.0 copy-done.6
  62.7 11.5 %add_maximum_fusion = f32[784,2048]{1,0:T(8,128)} fusion(bf16[784,2048]{1,0:T(8,128)(2,1)} %reshape.135, bf16[512,2048]{1,0:T(8,128)(2,1)S(1)} %copy-done, f32[2048]{0:T(1024)S(1)} %copy-done.3, f32[2048]{0:T(1024)S(1)} %copy-done.4, f32[784,512]{1,0:T(8,128)} %fusion.2, f32[784,512]{1,0:T(8,128)} %fusion.4, f32[784,512]{1,0:T(8,128)} %fusion.6, ...), kind=kOutput, calls=%fused_computation.3 | convolution fusion | flops 2068054016 | bytes 25923584 | tf_op jit(solution)/shard_map/dot_general | solution.py:73
  74.2 5.3 %reshape.145 = f32[16,49,2048]{2,1,0:T(8,128)} reshape(f32[784,2048]{1,0:T(8,128)} %add_maximum_fusion) | data formatting | bytes 12845056 | tf_op jit(solution)/shard_map/reshape | solution.py:79
  79.5 0.0 copy-start.9
  79.5 4.1 %reduce_sum.19 = f32[16,2048]{1,0:T(8,128)S(1)} reduce(f32[16,49,2048]{2,1,0:T(8,128)} %reshape.145, f32[]{:T(128)} %constant.38.clone.1), dimensions={1}, to_apply=%region_1.2 | reduce | flops 1572864 | bytes 6553604 | tf_op jit(solution)/shard_map/reduce_sum | solution.py:78
  84.3 0.0 copy-done.9
  84.3 0.6 dynamic-slice
  84.9 0.7 dynamic-update-slice
  85.7 29.6 %all-reduce.1 = s32[128]{0:T(128)S(1)} all-reduce(s32[128]{0:T(128)S(1)} %dynamic-update-slice), channel_id=2, replica_groups=mesh['grp'=4,'ext_0'=8,'ext_1'=4,'ext_2'=2] {'grp','ext_0','ext_1'}, use_global_device_ids=true, to_apply=%add.1 | all-reduce | flops 128 | bytes 1024
  115.3 1.8 %all-gather.2 = s32[2,1,128]{2,1,0:T(1,128)S(1)} all-gather(s32[1,1,128]{2,1,0:T(1,128)S(1)} %bitcast.56), channel_id=3, replica_groups=mesh['grp'=4,'ext_0'=8,'ext_1'=4,'ext_2'=2] {'ext_2'}, dimensions={0}, use_global_device_ids=true | all-gather | bytes 1536 | tf_op jit(solution)/shard_map/all_gather | solution.py:21
  117.1 0.7 fusion.28
  118.4 0.6 gather_fusion.1
  119.0 0.1 broadcast_select_fusion
  119.0 2.1 %collective-permute-start = (bf16[8,2048]{1,0:T(8,128)(2,1)S(1)}, bf16[8,2048]{1,0:T(8,128)(2,1)S(1)}, u32[]{:S(2)}, u32[]{:S(2)}) collective-permute-start(bf16[8,2048]{1,0:T(8,128)(2,1)S(1)} %broadcast_select_fusion), channel_id=1, source_target_pairs={{0,1},{1,2},{2,3},{3,4},{4,5},{5,6},{6,7},{7,8},{8,9},{9,10},{10,1... | collective-permute-start | bytes 98312 | tf_op jit(solution)/shard_map/ppermute | solution.py:35
  121.2 0.6 gather_fusion.2
  121.8 6.7 %collective-permute-done = bf16[8,2048]{1,0:T(8,128)(2,1)S(1)} collective-permute-done((bf16[8,2048]{1,0:T(8,128)(2,1)S(1)}, bf16[8,2048]{1,0:T(8,128)(2,1)S(1)}, u32[]{:S(2)}, u32[]{:S(2)}) %collective-permute-start) | collective-permute-done | bytes 32800 | tf_op jit(solution)/shard_map/ppermute | solution.py:35
  128.5 0.7 broadcast_select_fusion.1
  (9 shorter events, 0.1 us)
Async XLA Ops:
  0.0 62.7 %copy-start = (bf16[512,2048]{1,0:T(8,128)(2,1)S(1)}, bf16[512,2048]{1,0:T(8,128)(2,1)}, u32[]{:S(2)}) copy-start(bf16[512,2048]{1,0:T(8,128)(2,1)} %param.21) | copy-start | bytes 6291460
  5.6 3.8 %copy-start.7 = (f32[512]{0:T(512)S(1)}, f32[512]{0:T(512)}, u32[]{:S(2)}) copy-start(f32[512]{0:T(512)} %param.17) | copy-start | bytes 6148
  5.6 3.8 %copy-start.8 = (f32[512]{0:T(512)S(1)}, f32[512]{0:T(512)}, u32[]{:S(2)}) copy-start(f32[512]{0:T(512)} %param.16) | copy-start | bytes 6148
  13.8 0.9 copy-start.1
  24.4 3.1 %copy-start.2 = (bf16[784,512]{1,0:T(8,128)(2,1)S(1)}, bf16[784,512]{1,0:T(8,128)(2,1)}, u32[]{:S(2)}) copy-start(bf16[784,512]{1,0:T(8,128)(2,1)} %reshape.140) | copy-start | bytes 2408452
  58.4 4.3 %copy-start.3 = (f32[2048]{0:T(1024)S(1)}, f32[2048]{0:T(1024)}, u32[]{:S(2)}) copy-start(f32[2048]{0:T(1024)} %param.23) | copy-start | bytes 24580
  58.4 4.3 %copy-start.4 = (f32[2048]{0:T(1024)S(1)}, f32[2048]{0:T(1024)}, u32[]{:S(2)}) copy-start(f32[2048]{0:T(1024)} %param.22) | copy-start | bytes 24580
  58.4 4.3 %copy-start.5 = (f32[512]{0:T(512)S(1)}, f32[512]{0:T(512)}, u32[]{:S(2)}) copy-start(f32[512]{0:T(512)} %param.20) | copy-start | bytes 6148
  58.4 4.3 %copy-start.6 = (f32[512]{0:T(512)S(1)}, f32[512]{0:T(512)}, u32[]{:S(2)}) copy-start(f32[512]{0:T(512)} %param.19) | copy-start | bytes 6148
  79.5 4.8 %copy-start.9 = (u32[256]{0:T(256)S(1)}, u32[256]{0:T(256)}, u32[]{:S(2)}) copy-start(u32[256]{0:T(256)} %constant.50) | copy-start | bytes 3076
  119.0 9.4 %collective-permute-start = (bf16[8,2048]{1,0:T(8,128)(2,1)S(1)}, bf16[8,2048]{1,0:T(8,128)(2,1)S(1)}, u32[]{:S(2)}, u32[]{:S(2)}) collective-permute-start(bf16[8,2048]{1,0:T(8,128)(2,1)S(1)} %broadcast_select_fusion), channel_id=1, source_target_pairs={{0,1},{1,2},{2,3},{3,4},{4,5},{5,6},{6,7},{7,8},{8,9},{9,10},{10,1... | collective-permute-start | bytes 98312 | tf_op jit(solution)/shard_map/ppermute | solution.py:35
where the time goes:
time: 130 us; the launch traced here: 129 us
  local copies, waits for them, and re-layouts  41.1 us (32%)
  matrix products  40 us (31%)
  blocking collectives  31.4 us (24%)
  waiting for transfers between devices  6.71 us (5%)
  other arithmetic  6.41 us (5%)
  starting transfers between devices  2.1 us (2%)
  between operations  1.41 us (1%)
    unnamed x1, blocking collectives  29.6 us
    dot_general x8, matrix products, bottleneck(): jnp.dot(window, w_spatial[row_shift, col_shift], preferred_element_type=j...  24.1 us
    reshape x8, local copies, waits for them, and re-layouts, bottleneck(): window = padded[:, row_shift:row_shift + side_cells, col_shift:col_shift...  16.4 us
    dot_general x1, matrix products, bottleneck(): jnp.dot(spatial, w_expand, preferred_element_type=jnp.float32)  11.5 us
    ppermute x1, waiting for transfers between devices, passed_along(): return lax.ppermute(x, axis, pairs)  6.71 us
    slice x1, local copies, waits for them, and re-layouts, bottleneck(): padded[:, row_shift:row_shift + side_cells, col_shift:col_shift + side_ce...  6.34 us
    reshape x1, local copies, waits for them, and re-layouts, bottleneck(): expanded.reshape(count_tiles, side_cells * side_cells, channels)  5.27 us
    gather x1, local copies, waits for them, and re-layouts, on_device(): home_rows = bottleneck(tiles[listing[:2 * shard_rows]], *weights)  4.73 us
  transfers between devices with their start and end apart: 1, of which 1 were waited for; matrix products, arithmetic and copies ran while one was open for 0% of the time, Pallas kernels for 0%

commit v1 on v0

v1 whole, which is shorter than its diff:
```python
import functools

import jax
import jax.numpy as jnp
from jax import lax
from jax.experimental import pallas as pl
from jax.experimental.pallas import tpu as pltpu
from jax.sharding import PartitionSpec as P

MESH = pl.DeviceIdType.MESH
SIDE = 7
CELLS = SIDE * SIDE
HALF = 8
SLOTS = 2 * HALF
BODY = 48
ROWS = SLOTS * CELLS
KC = 1024
NC = 256


def dot(a, b):
    return jnp.dot(a, b, preferred_element_type=jnp.float32)


def kernel(
    comm,
    groups,
    planes,
    ti,
    tc,
    x_hbm,
    wr_hbm,
    sr,
    br,
    ws_hbm,
    ss,
    bs,
    we_hbm,
    se,
    be,
    out,
    x,
    wr,
    ws,
    we,
    xs,
    last,
    red,
    cin,
    acc,
    spat,
    tail,
    own,
    spill,
    arrived,
    cnt,
    got1,
    got2,
    got3,
    x_sem,
    wr_sem,
    ws_sem,
    we_sem,
    send1,
    recv1,
    send2,
    recv2,
    send3,
    recv3,
    spill_send,
    spill_recv,
):
    channels = x_hbm.shape[2]
    inner = wr_hbm.shape[1]
    chunks = channels // KC
    bf16 = jnp.bfloat16
    f32 = jnp.float32

    copies_x = []
    copies_r = []
    for k in range(chunks):
        at = pl.ds(k * KC, KC)
        cx = pltpu.make_async_copy(x_hbm.at[:, :, at], x[k], x_sem.at[k])
        cr = pltpu.make_async_copy(wr_hbm.at[at], wr.at[at], wr_sem.at[k])
        cx.start()
        cr.start()
        copies_x.append(cx)
        copies_r.append(cr)
    copies_s = {}
    for a in (1, 0, 2):
        cs = pltpu.make_async_copy(ws_hbm.at[a], ws.at[a], ws_sem.at[a])
        cs.start()
        copies_s[a] = cs
    ce = pltpu.make_async_copy(we_hbm, we, we_sem)
    ce.start()

    count = tc[0]
    if comm:
        g = lax.axis_index("grp")
        e = lax.axis_index("ext")
        ext = lax.axis_size("ext")
        plane = ext // planes
        p = e // plane
        q = lax.rem(e, plane)
        rank = g * ext + e
        total = groups * ext
        ahead = lax.rem(rank + 1, total)
        behind = lax.rem(rank + total - 1, total)

        def device(r):
            return (r // ext, lax.rem(r, ext))

        near = [lax.rem(q + k, plane) for k in range(1, plane)]
        far = [lax.rem(p + k, planes) for k in range(1, planes)]
        wide = [lax.rem(g + k, groups) for k in range(1, groups)]
        barrier = pltpu.get_barrier_semaphore()
        greeted = (
            [(g, p * plane + o) for o in near]
            + [(g, o * plane + q) for o in far]
            + [(o, e) for o in wide]
            + [device(behind)]
        )
        for who in greeted:
            pl.semaphore_signal(barrier, inc=1, device_id=who, device_id_type=MESH)

    def start(me, others, ids, where, box, send, recv):
        started = []
        for k, who in enumerate(ids):
            c = pltpu.make_async_remote_copy(
                src_ref=cnt.at[where],
                dst_ref=box.at[me],
                send_sem=send.at[k],
                recv_sem=recv.at[me],
                device_id=who,
                device_id_type=MESH,
            )
            c.start()
            started.append(c)
        return started

    def finish(me, others, ids, where, box, send, recv):
        before = jnp.zeros((1, 128), jnp.int32)
        whole = cnt[where]
        for k, (o, who) in enumerate(zip(others, ids)):
            pltpu.make_async_remote_copy(
                src_ref=cnt.at[where],
                dst_ref=box.at[o],
                send_sem=send.at[k],
                recv_sem=recv.at[o],
                device_id=who,
                device_id_type=MESH,
            ).wait()
            value = box[o]
            whole = whole + value
            before = before + jnp.where(o < me, value, 0)
        return before, whole

    slots = [jnp.clip(count - HALF + j, 0, SLOTS - 1) for j in range(HALF)]
    slots = slots + list(range(HALF))
    idx = [ti[0, s] for s in slots]

    for k in range(chunks):
        at = pl.ds(k * KC, KC)
        copies_x[k].wait()
        for s in range(SLOTS):
            xs[s * BODY : (s + 1) * BODY, at] = x[k][idx[s], 0:BODY, :]
            last[s : s + 1, at] = x[k][idx[s], BODY:CELLS, :].astype(f32)
        xs[SLOTS * BODY : ROWS, at] = last[:, at].astype(bf16)
        copies_r[k].wait()
        for m0, m1 in ((0, 256), (256, 512), (512, ROWS)):
            part = dot(xs[m0:m1, at], wr[at, :])
            if k > 0:
                part = part + acc[m0:m1]
            if k < chunks - 1:
                acc[m0:m1] = part
            else:
                red[m0:m1] = jnp.maximum(
                    part * sr[...][None, :] + br[...][None, :], 0.0
                ).astype(bf16)

    if comm:
        pl.semaphore_wait(barrier, len(greeted))
        cnt[0] = jnp.full((1, 128), count, jnp.int32)
        args1 = (q, near, [(g, p * plane + o) for o in near], 0, got1, send1, recv1)
        start(*args1)

    r = lax.broadcasted_iota(jnp.int32, (256, 256), 0)
    c = lax.broadcasted_iota(jnp.int32, (256, 256), 1)
    swap = jnp.where(
        (r // SLOTS == lax.rem(c, SLOTS)) & (lax.rem(r, SLOTS) == c // SLOTS), 1.0, 0.0
    ).astype(bf16)
    zero = jnp.zeros((SLOTS, inner), bf16)
    for i in range(SIDE):
        cin[i, 0] = zero
        cin[i, SIDE + 1] = zero
    for b in range(3):
        block = jnp.concatenate(
            [red[s * BODY + b * 16 : s * BODY + b * 16 + 16] for s in range(SLOTS)], axis=0
        )
        turned = dot(swap, block).astype(bf16)
        for t in range(16):
            cell = b * 16 + t
            cin[cell // SIDE, cell % SIDE + 1] = turned[t * SLOTS : (t + 1) * SLOTS]
    cin[SIDE - 1, SIDE] = red[SLOTS * BODY : ROWS]

    for a in (1, 0, 2):
        copies_s[a].wait()
        lo, hi = max(0, 1 - a), min(SIDE, SIDE + 1 - a)
        for i0, i1 in ((0, 2), (2, 4), (4, 7)):
            j0, j1 = max(i0, lo), min(i1, hi)
            m = (j1 - j0) * SIDE * SLOTS
            part = None
            for b in range(3):
                lhs = cin[j0 + a - 1 : j1 + a - 1, b : b + SIDE].reshape(m, inner)
                d = dot(lhs, ws[a, b])
                part = d if part is None else part + d
            o0, o1 = j0 * SIDE * SLOTS, j1 * SIDE * SLOTS
            if a == 1:
                acc[o0:o1] = part
            else:
                acc[o0:o1] = acc[o0:o1] + part
        if comm and a == 1:
            before1, whole1 = finish(*args1)
            cnt[1] = whole1
            args2 = (p, far, [(g, o * plane + q) for o in far], 1, got2, send2, recv2)
            start(*args2)
        if comm and a == 0:
            before2, whole2 = finish(*args2)
            cnt[2] = whole2
            args3 = (g, wide, [(o, e) for o in wide], 2, got3, send3, recv3)
            start(*args3)

    sp = lambda m0, m1: jnp.maximum(
        acc[m0:m1] * ss[...][None, :] + bs[...][None, :], 0.0
    ).astype(bf16)
    for b in range(3):
        turned = dot(swap, sp(b * 256, (b + 1) * 256)).astype(bf16)
        for s in range(SLOTS):
            spat[s * BODY + b * 16 : s * BODY + b * 16 + 16] = turned[s * 16 : s * 16 + 16]
    spat[SLOTS * BODY : ROWS] = sp(SLOTS * BODY, ROWS)

    ce.wait()

    def expanded(m0, m1, at):
        v = dot(spat[m0:m1], we[:, at]) * se[at][None, :] + be[at][None, :]
        return jnp.maximum(v + xs[m0:m1, at].astype(f32), 0.0)

    for half in range(2):
        for n in range(channels // NC):
            at = pl.ds(n * NC, NC)
            if half == 0:
                tail[:, at] = expanded(SLOTS * BODY, ROWS, at)
            v = expanded(half * HALF * BODY, (half + 1) * HALF * BODY, at)
            v = jnp.sum(v.reshape(HALF, BODY, NC), axis=1)
            v = (v + tail[half * HALF : (half + 1) * HALF, at]) * (1.0 / CELLS)
            if half == 0:
                spill[:, at] = v.astype(bf16)
            else:
                own[:, at] = v.astype(bf16)
        if half == 0 and comm:
            moved = pltpu.make_async_remote_copy(
                src_ref=spill,
                dst_ref=arrived,
                send_sem=spill_send,
                recv_sem=spill_recv,
                device_id=device(ahead),
                device_id_type=MESH,
            )
            moved.start()

    if comm:
        before3, _ = finish(*args3)
        backlog = before1 + before2 + before3 - rank * HALF
        moved.wait()
        prior = arrived[...]
    else:
        backlog = jnp.full((1, 128), 3, jnp.int32)
        prior = spill[...]
    both = jnp.concatenate([prior.astype(f32), own[...].astype(f32)], axis=0).astype(bf16)
    row = lax.broadcasted_iota(jnp.int32, (HALF, SLOTS), 0)
    col = lax.broadcasted_iota(jnp.int32, (HALF, SLOTS), 1)
    pick = jnp.where(col - row == HALF - backlog[:, :SLOTS], 1.0, 0.0).astype(bf16)
    out[...] = dot(pick, both).astype(bf16)


def on_device(comm, groups, planes, tiles, tissue_index, tissue_count, wr, sr, br, ws, ss, bs, we, se, be):
    cand, cells, channels = tiles.shape
    inner = wr.shape[1]
    plane = lax.axis_size("ext") // planes if comm else 8
    smem = pl.BlockSpec(memory_space=pltpu.SMEM)
    vmem = pl.BlockSpec(memory_space=pltpu.VMEM)
    hbm = pl.BlockSpec(memory_space=pl.ANY)
    bf16 = jnp.bfloat16
    f32 = jnp.float32
    dma = pltpu.SemaphoreType.DMA
    return pl.pallas_call(
        functools.partial(kernel, comm, groups, planes),
        out_shape=jax.ShapeDtypeStruct((HALF, channels), bf16),
        in_specs=[smem, smem, hbm, hbm, vmem, vmem, hbm, vmem, vmem, hbm, vmem, vmem],
        out_specs=vmem,
        scratch_shapes=[
            [pltpu.VMEM((cand, cells, KC), bf16)] * (channels // KC),
            pltpu.VMEM((channels, inner), bf16),
            pltpu.VMEM((3, 3, inner, inner), bf16),
            pltpu.VMEM((inner, channels), bf16),
            pltpu.VMEM((ROWS, channels), bf16),
            pltpu.VMEM((SLOTS, channels), f32),
            pltpu.VMEM((ROWS, inner), bf16),
            pltpu.VMEM((SIDE, SIDE + 2, SLOTS, inner), bf16),
            pltpu.VMEM((ROWS, inner), f32),
            pltpu.VMEM((ROWS, inner), bf16),
            pltpu.VMEM((SLOTS, channels), f32),
            pltpu.VMEM((HALF, channels), bf16),
            pltpu.VMEM((HALF, channels), bf16),
            pltpu.VMEM((HALF, channels), bf16),
            pltpu.VMEM((3, 1, 128), jnp.int32),
            pltpu.VMEM((plane, 1, 128), jnp.int32),
            pltpu.VMEM((planes, 1, 128), jnp.int32),
            pltpu.VMEM((groups, 1, 128), jnp.int32),
            dma((channels // KC,)),
            dma((channels // KC,)),
            dma((3,)),
            dma,
            dma((plane - 1,)),
            dma((plane,)),
            dma((planes - 1,)),
            dma((planes,)),
            dma((groups - 1,)),
            dma((groups,)),
            dma,
            dma,
        ],
        compiler_params=pltpu.CompilerParams(
            collective_id=0 if comm else None,
            has_side_effects=True,
            vmem_limit_bytes=56 * 1024 * 1024,
        ),
        name="bottleneck",
    )(tissue_index, tissue_count, tiles, wr, sr, br, ws, ss, bs, we, se, be)


def solution(mesh):
    axes = ("grp", "ext")
    split = P(axes)
    return jax.shard_map(
        functools.partial(on_device, True, mesh.shape["grp"], 8),
        mesh=mesh,
        in_specs=(split, split, split) + (P(),) * 9,
        out_specs=split,
        check_vma=False,
    )
```

time: 130 us -> 27.7 us (0.21)
  the two profiles are of different devices: /device:TPU:8 before, /device:TPU:1 now
where the time goes in v1:
time: 27.7 us; the launch traced here: 27.5 us
  Pallas kernels  25.5 us (92%)
  local copies, waits for them, and re-layouts  1.38 us (5%)
  between operations  0.66 us (2%)
    pallas_call x1, Pallas kernels, on_device(): pl.pallas_call(functools.partial(kernel, comm, groups, planes), out_shape...  25.5 us
    unnamed x1, local copies, waits for them, and re-layouts  1.38 us

profile of v1, /device:TPU:1, one launch (start us, length us, event | category | flops | bytes accessed | tf_op | source)
XLA Modules:
  0.0 27.5 jit_solution(16137694147656104566)
XLA Ops:
  0.7 25.5 %bottleneck.1 = bf16[8,2048]{1,0:T(8,128)(2,1)} custom-call(s32[1,18]{1,0:T(1,128)} %ti.1, s32[1]{0:T(128)S(6)} %copy.14.tc, bf16[18,49,2048]{2,1,0:T(8,128)(2,1)} %x_hbm.1, bf16[2048,512]{1,0:T(8,128)(2,1)} %wr_hbm.1, f32[512]{0:T(512)} %sr.1, f32[512]{0:T(512)} %br.1, bf16[3,3,512,512]{3,2,1,0:T(8,128)(2,1)} %ws_hbm.1, f32[512]{0:T(512)} %ss.1, f32[512]{0:T(512)} %bs.1, ...), custom_call_target="tpu_custom_call" | custom-call | tf_op jit(solution)/shard_map/bottleneck/pallas_call | solution.py:296
  26.1 1.4 %copy.15 = bf16[8,2048]{1,0:T(8,128)(2,1)} copy(bf16[8,2048]{1,0:T(8,128)(2,1)} %bottleneck.1) | data formatting | bytes 65536

commit v2 on v1

v2 whole, which is shorter than its diff:
```python
import functools

import jax
import jax.numpy as jnp
from jax import lax
from jax.experimental import pallas as pl
from jax.experimental.pallas import tpu as pltpu
from jax.sharding import PartitionSpec as P

MESH = pl.DeviceIdType.MESH
SIDE = 7
CELLS = SIDE * SIDE
HALF = 8
SLOTS = 2 * HALF
BODY = 48
ROWS = HALF * BODY
FULL = ROWS + HALF
FOLD = 4
KC = 1024
NC = 256
TEAM = 16
LANES = 128
bf16 = jnp.bfloat16
f32 = jnp.float32


def dot(a, b):
    return jnp.dot(a, b, preferred_element_type=jnp.float32)


class Exchange:
    def __init__(self, groups, cnt, got1, got2, send1, recv1, send2, recv2):
        self.cnt, self.boxes = cnt, (got1, got2)
        self.sends, self.recvs = (send1, send2), (recv1, recv2)
        g = lax.axis_index("grp")
        e = lax.axis_index("ext")
        ext = lax.axis_size("ext")
        per = ext // TEAM
        self.teams = groups * per
        self.rank = g * ext + e
        total = groups * ext
        self.device = lambda r: (r // ext, lax.rem(r, ext))
        team = self.rank // TEAM
        seat = lax.rem(self.rank, TEAM)
        seats = [lax.rem(seat + k, TEAM) for k in range(1, TEAM)]
        others = [lax.rem(team + k, self.teams) for k in range(1, self.teams)]
        self.me = (seat, team)
        self.peers = (seats, others)
        self.ids = (
            [self.device(team * TEAM + o) for o in seats],
            [self.device(o * TEAM + seat) for o in others],
        )
        self.ahead = self.device(lax.rem(self.rank + 1, total))
        behind = self.device(lax.rem(self.rank + total - 1, total))
        self.greeted = self.ids[0] + self.ids[1] + [behind]
        self.layer = lax.rem(e // (ext // 8), 8)

    def greet(self):
        barrier = pltpu.get_barrier_semaphore()
        for who in self.greeted:
            pl.semaphore_signal(barrier, inc=1, device_id=who, device_id_type=MESH)

    def enter(self):
        pl.semaphore_wait(pltpu.get_barrier_semaphore(), len(self.greeted))

    def start(self, stage):
        for k, who in enumerate(self.ids[stage]):
            pltpu.make_async_remote_copy(
                src_ref=self.cnt.at[stage],
                dst_ref=self.boxes[stage].at[self.me[stage]],
                send_sem=self.sends[stage].at[k],
                recv_sem=self.recvs[stage].at[self.me[stage]],
                device_id=who,
                device_id_type=MESH,
            ).start()

    def finish(self, stage):
        before = jnp.zeros((1, 128), jnp.int32)
        whole = self.cnt[stage]
        for k, (o, who) in enumerate(zip(self.peers[stage], self.ids[stage])):
            pltpu.make_async_remote_copy(
                src_ref=self.cnt.at[stage],
                dst_ref=self.boxes[stage].at[o],
                send_sem=self.sends[stage].at[k],
                recv_sem=self.recvs[stage].at[o],
                device_id=who,
                device_id_type=MESH,
            ).wait()
            value = self.boxes[stage][o]
            whole = whole + value
            before = before + jnp.where(o < self.me[stage], value, 0)
        return before, whole


def kernel(
    comm,
    groups,
    ti,
    tc,
    x_hbm,
    wr_hbm,
    sr,
    br,
    ws_hbm,
    ss,
    bs,
    we_hbm,
    se,
    be,
    out,
    x,
    wr,
    ws,
    we,
    xs,
    last,
    acc,
    flat,
    cin,
    spat,
    own,
    spill,
    arrived,
    cnt,
    base,
    got1,
    got2,
    x_sem,
    wr_sem,
    ws_sem,
    we_sem,
    send1,
    recv1,
    send2,
    recv2,
    spill_send,
    spill_recv,
):
    channels = x_hbm.shape[2]
    inner = wr_hbm.shape[1]
    chunks = channels // KC

    if comm:
        ex = Exchange(groups, cnt, got1, got2, send1, recv1, send2, recv2)
        ex.greet()

    copies_x = []
    copies_r = []
    for k in range(chunks):
        at = pl.ds(k * KC, KC)
        cx = pltpu.make_async_copy(x_hbm.at[:, :, at], x[k], x_sem.at[k])
        cr = pltpu.make_async_copy(wr_hbm.at[at], wr.at[at], wr_sem.at[k])
        cx.start()
        cr.start()
        copies_x.append(cx)
        copies_r.append(cr)
    copies_s = []
    for a in range(3):
        cs = pltpu.make_async_copy(ws_hbm.at[a], ws.at[a], ws_sem.at[a])
        cs.start()
        copies_s.append(cs)
    ce = pltpu.make_async_copy(we_hbm, we, we_sem)
    ce.start()

    count = tc[0]
    if comm:
        cnt[0] = jnp.full((1, 128), count, jnp.int32)

    def site(place):
        if not comm:
            return
        early, middle = ex.layer < 2, (ex.layer >= 2) & (ex.layer < 5)
        late = ex.layer >= 5
        first = {0: late, 2: middle, 4: early}
        second = {1: late, 3: middle, 5: early}
        if place in first:

            @pl.when(first[place])
            def _():
                ex.enter()
                ex.start(0)
                if place > 0:
                    send_spill()

        if place in second:

            @pl.when(second[place])
            def _():
                before, whole = ex.finish(0)
                base[...] = before
                cnt[1] = whole
                ex.start(1)

        if place == 2:

            @pl.when(late)
            def _():
                send_spill()

    def moved():
        return pltpu.make_async_remote_copy(
            src_ref=spill,
            dst_ref=arrived,
            send_sem=spill_send,
            recv_sem=spill_recv,
            device_id=ex.ahead,
            device_id_type=MESH,
        )

    def send_spill():
        moved().start()

    for half in range(2):
        if half == 0:
            slots = [jnp.clip(count - HALF + j, 0, SLOTS - 1) for j in range(HALF)]
        else:
            slots = list(range(HALF))
        idx = [ti[0, s] for s in slots]

        for k in range(chunks):
            at = pl.ds(k * KC, KC)
            if half == 0:
                copies_x[k].wait()
            for s in range(HALF):
                xs[half, s * BODY : (s + 1) * BODY, at] = x[k][idx[s], 0:BODY, :]
                last[s : s + 1, at] = x[k][idx[s], BODY:CELLS, :].astype(f32)
            xs[half, ROWS:FULL, at] = last[:, at].astype(bf16)
            if half == 0:
                copies_r[k].wait()
            part = dot(xs[half, :, at], wr[at, :])
            if k > 0:
                part = part + acc[0:FULL]
            if k < chunks - 1:
                acc[0:FULL] = part
            else:
                part = jnp.maximum(part * sr[...][None, :] + br[...][None, :], 0.0)
                for j in range(inner // LANES):
                    flat[j] = part[:, j * LANES : (j + 1) * LANES]
        site(3 * half)

        def cell(i, k):
            c = i * SIDE + k
            if i >= SIDE:
                return jnp.zeros((HALF, inner), f32)
            if c == BODY:
                parts = [flat[j, ROWS:FULL, :] for j in range(inner // LANES)]
            else:
                at = pl.ds(c, HALF, stride=BODY)
                parts = [flat[j, at, :] for j in range(inner // LANES)]
            return jnp.concatenate(parts, axis=1)

        none = jnp.zeros((HALF, inner), f32)
        if half == 0:
            for i in range(FOLD + 2):
                cin[i, 0] = jnp.zeros((SLOTS, inner), bf16)
                cin[i, SIDE + 1] = jnp.zeros((SLOTS, inner), bf16)
        for k in range(SIDE):
            for i in range(FOLD):
                low, high = cell(i, k), cell(i + FOLD, k)
                cin[i + 1, k + 1] = jnp.concatenate([low, high], axis=0).astype(bf16)
                if i == FOLD - 1:
                    cin[0, k + 1] = jnp.concatenate([none, low], axis=0).astype(bf16)
                if i == 0:
                    cin[FOLD + 1, k + 1] = jnp.concatenate([high, none], axis=0).astype(bf16)

        for a in range(3):
            if half == 0:
                copies_s[a].wait()
            lhs = jnp.concatenate(
                [
                    cin[a : a + FOLD, b : b + SIDE].reshape(FOLD * SIDE * SLOTS, inner)
                    for b in range(3)
                ],
                axis=1,
            )
            part = dot(lhs, ws[a].reshape(3 * inner, inner))
            if a > 0:
                part = part + acc[...]
            if a < 2:
                acc[...] = part
            else:
                part = jnp.maximum(part * ss[...][None, :] + bs[...][None, :], 0.0)
                for i in range(FOLD):
                    for k in range(SIDE):
                        v = (i * SIDE + k) * SLOTS
                        for up in range(2):
                            c = (i + up * FOLD) * SIDE + k
                            piece = part[v + up * HALF : v + up * HALF + HALF]
                            for j in range(inner // LANES):
                                strip = piece[:, j * LANES : (j + 1) * LANES]
                                if c < BODY:
                                    flat[j, pl.ds(c, HALF, stride=BODY), :] = strip
                                elif c == BODY:
                                    flat[j, ROWS:FULL, :] = strip
        for j in range(inner // LANES):
            spat[:, j * LANES : (j + 1) * LANES] = flat[j].astype(bf16)
        site(3 * half + 1)

        if half == 0:
            ce.wait()
        for n in range(channels // NC):
            at = pl.ds(n * NC, NC)
            v = dot(spat[...], we[:, at]) * se[at][None, :] + be[at][None, :]
            v = jnp.maximum(v + xs[half, :, at].astype(f32), 0.0)
            v = jnp.sum(v[:ROWS].reshape(HALF, BODY, NC), axis=1) + v[ROWS:FULL]
            v = (v * (1.0 / CELLS)).astype(bf16)
            if half == 0:
                spill[:, at] = v
            else:
                own[:, at] = v
        site(3 * half + 2)

    if comm:
        before, _ = ex.finish(1)
        backlog = base[...] + before - ex.rank * HALF
        moved().wait()
        prior = arrived[...]
    else:
        backlog = jnp.full((1, 128), 3, jnp.int32)
        prior = spill[...]
    both = jnp.concatenate([prior.astype(f32), own[...].astype(f32)], axis=0).astype(bf16)
    row = lax.broadcasted_iota(jnp.int32, (HALF, SLOTS), 0)
    col = lax.broadcasted_iota(jnp.int32, (HALF, SLOTS), 1)
    pick = jnp.where(col - row == HALF - backlog[:, :SLOTS], 1.0, 0.0).astype(bf16)
    out[...] = dot(pick, both).astype(bf16)


def on_device(comm, groups, tiles, tissue_index, tissue_count, wr, sr, br, ws, ss, bs, we, se, be):
    cand, cells, channels = tiles.shape
    inner = wr.shape[1]
    teams = groups * (lax.axis_size("ext") // TEAM) if comm else 16
    smem = pl.BlockSpec(memory_space=pltpu.SMEM)
    vmem = pl.BlockSpec(memory_space=pltpu.VMEM)
    hbm = pl.BlockSpec(memory_space=pl.ANY)
    dma = pltpu.SemaphoreType.DMA
    return pl.pallas_call(
        functools.partial(kernel, comm, groups),
        out_shape=jax.ShapeDtypeStruct((HALF, channels), bf16),
        in_specs=[smem, smem, hbm, hbm, vmem, vmem, hbm, vmem, vmem, hbm, vmem, vmem],
        out_specs=vmem,
        scratch_shapes=[
            [pltpu.VMEM((cand, cells, KC), bf16)] * (channels // KC),
            pltpu.VMEM((channels, inner), bf16),
            pltpu.VMEM((3, 3, inner, inner), bf16),
            pltpu.VMEM((inner, channels), bf16),
            pltpu.VMEM((2, FULL, channels), bf16),
            pltpu.VMEM((HALF, channels), f32),
            pltpu.VMEM((FOLD * SIDE * SLOTS, inner), f32),
            pltpu.VMEM((inner // LANES, FULL, LANES), f32),
            pltpu.VMEM((FOLD + 2, SIDE + 2, SLOTS, inner), bf16),
            pltpu.VMEM((FULL, inner), bf16),
            pltpu.VMEM((HALF, channels), bf16),
            pltpu.VMEM((HALF, channels), bf16),
            pltpu.VMEM((HALF, channels), bf16),
            pltpu.VMEM((2, 1, 128), jnp.int32),
            pltpu.VMEM((1, 128), jnp.int32),
            pltpu.VMEM((TEAM, 1, 128), jnp.int32),
            pltpu.VMEM((teams, 1, 128), jnp.int32),
            dma((channels // KC,)),
            dma((channels // KC,)),
            dma((3,)),
            dma,
            dma((TEAM - 1,)),
            dma((TEAM,)),
            dma((teams - 1,)),
            dma((teams,)),
            dma,
            dma,
        ],
        compiler_params=pltpu.CompilerParams(
            collective_id=0 if comm else None,
            has_side_effects=True,
            vmem_limit_bytes=56 * 1024 * 1024,
        ),
        name="bottleneck",
    )(tissue_index, tissue_count, tiles, wr, sr, br, ws, ss, bs, we, se, be)


def solution(mesh):
    axes = ("grp", "ext")
    split = P(axes)
    return jax.shard_map(
        functools.partial(on_device, True, mesh.shape["grp"]),
        mesh=mesh,
        in_specs=(split, split, split) + (P(),) * 9,
        out_specs=split,
        check_vma=False,
    )
```

time: 27.7 us -> 29.8 us (1.076)
  Pallas kernels: 25.5 us -> 27.6 us
    pallas_call x1, Pallas kernels: 25.5 us -> 27.6 us  [on_device(): pl.pallas_call(functools.partial(kernel, comm, groups), out_shape=jax.Sha...]
where the time goes in v2:
time: 29.8 us; the launch traced here: 29.6 us
  Pallas kernels  27.6 us (93%)
  local copies, waits for them, and re-layouts  1.38 us (5%)
  between operations  0.66 us (2%)
    pallas_call x1, Pallas kernels, on_device(): pl.pallas_call(functools.partial(kernel, comm, groups), out_shape=jax.Sha...  27.6 us
    unnamed x1, local copies, waits for them, and re-layouts  1.38 us

profile of v2, /device:TPU:1, one launch (start us, length us, event | category | flops | bytes accessed | tf_op | source)
XLA Modules:
  0.0 29.6 jit_solution(3881645823202640366)
XLA Ops:
  0.7 27.6 %bottleneck.1 = bf16[8,2048]{1,0:T(8,128)(2,1)} custom-call(s32[1,18]{1,0:T(1,128)} %ti.1, s32[1]{0:T(128)S(6)} %copy.14.tc, bf16[18,49,2048]{2,1,0:T(8,128)(2,1)} %x_hbm.1, bf16[2048,512]{1,0:T(8,128)(2,1)} %wr_hbm.1, f32[512]{0:T(512)} %sr.1, f32[512]{0:T(512)} %br.1, bf16[3,3,512,512]{3,2,1,0:T(8,128)(2,1)} %ws_hbm.1, f32[512]{0:T(512)} %ss.1, f32[512]{0:T(512)} %bs.1, ...), custom_call_target="tpu_custom_call" | custom-call | tf_op jit(solution)/shard_map/bottleneck/pallas_call | solution.py:336
  28.2 1.4 %copy.15 = bf16[8,2048]{1,0:T(8,128)(2,1)} copy(bf16[8,2048]{1,0:T(8,128)(2,1)} %bottleneck.1) | data formatting | bytes 65536

commit v3 on v2

v3 whole, which is shorter than its diff:
```python
import functools

import jax
import jax.numpy as jnp
from jax import lax
from jax.experimental import pallas as pl
from jax.experimental.pallas import tpu as pltpu
from jax.sharding import PartitionSpec as P

MESH = pl.DeviceIdType.MESH
SIDE = 7
CELLS = SIDE * SIDE
HALF = 8
SLOTS = 2 * HALF
BODY = 48
ROWS = HALF * BODY
FULL = ROWS + HALF
FOLD = 4
KC = 1024
NC = 256
LAYERS = 8
ROW = 8
LANES = 128
bf16 = jnp.bfloat16
f32 = jnp.float32


def dot(a, b):
    return jnp.dot(a, b, preferred_element_type=jnp.float32)


class Exchange:
    def __init__(self, groups, cnt, box, table, tables, answer, sems):
        self.cnt, self.box, self.table, self.tables, self.answer = cnt, box, table, tables, answer
        self.post_send, self.post_recv, self.row_send, self.row_recv, self.out_send, self.out_recv = sems
        self.groups = groups
        g = self.g = lax.axis_index("grp")
        e = lax.axis_index("ext")
        ext = lax.axis_size("ext")
        self.z = e // ROW
        self.q = lax.rem(e, ROW)
        self.rank = g * ext + e
        total = groups * ext
        self.hub = self.z == 0
        after = lax.rem(self.rank + 1, total)
        before = lax.rem(self.rank + total - 1, total)
        self.ahead = (after // ext, lax.rem(after, ext))
        self.behind = (before // ext, lax.rem(before, ext))
        self.far = [lax.rem(g + k, groups) for k in range(groups)]
        self.mates = [lax.rem(self.q + k, ROW) for k in range(1, ROW)]

    def greet(self):
        barrier = pltpu.get_barrier_semaphore()

        def tell(who):
            pl.semaphore_signal(barrier, inc=1, device_id=who, device_id_type=MESH)

        @pl.when(self.hub)
        def _():
            for z in reversed(range(LAYERS)):
                for k, y in enumerate(self.far):
                    if z > 0 or k > 0:
                        tell((y, z * ROW + self.q))
            for o in self.mates:
                tell((self.g, o))

        @pl.when(jnp.logical_not(self.hub))
        def _():
            tell((self.g, self.q))

        tell(self.behind)

    def to_hub(self, k, y):
        mine = self.g * LAYERS + self.z
        return pltpu.make_async_remote_copy(
            src_ref=self.cnt,
            dst_ref=self.box.at[mine],
            send_sem=self.post_send.at[k],
            recv_sem=self.post_recv,
            device_id=(y, self.q),
            device_id_type=MESH,
        )

    def post(self, hub):
        barrier = pltpu.get_barrier_semaphore()
        if hub:
            pl.semaphore_wait(barrier, self.groups - 1 + ROW - 1 + LAYERS - 1 + 1)
        else:
            pl.semaphore_wait(barrier, self.groups + 1)
        for k, y in enumerate(self.far):
            if not hub or k > 0:
                self.to_hub(k, y).start()

    def sent(self, hub):
        for k, y in enumerate(self.far):
            if not hub or k > 0:
                self.to_hub(k, y).wait_send()

    def all_of(self, box, sem):
        rows = box.at[pl.ds(0, box.shape[0] - 1)]
        pltpu.make_async_copy(rows, rows, sem).wait()

    def collect(self):
        self.all_of(self.box, self.post_recv)
        self.box[self.g * LAYERS] = self.cnt[...]
        lower = jnp.zeros((1, 128), jnp.int32)
        for y in range(self.groups):
            plane = self.box[y * LAYERS]
            for z in range(1, LAYERS):
                plane = plane + self.box[y * LAYERS + z]
            lower = lower + jnp.where(y < self.g, plane, 0)
        for z in range(LAYERS):
            self.table[z] = self.box[self.g * LAYERS + z]
        self.table[LAYERS] = lower
        for k, o in enumerate(self.mates):
            self.to_mate(k, o).start()

    def to_mate(self, k, o):
        return pltpu.make_async_remote_copy(
            src_ref=self.table,
            dst_ref=self.tables.at[self.q],
            send_sem=self.row_send.at[k],
            recv_sem=self.row_recv,
            device_id=(self.g, o),
            device_id_type=MESH,
        )

    def to_plane(self, z):
        return pltpu.make_async_remote_copy(
            src_ref=self.answer.at[z],
            dst_ref=self.answer.at[0],
            send_sem=self.out_send.at[z - 1],
            recv_sem=self.out_recv,
            device_id=(self.g, z * ROW + self.q),
            device_id_type=MESH,
        )

    def settle(self):
        self.all_of(self.tables, self.row_recv)
        for k, o in enumerate(self.mates):
            self.to_mate(k, o).wait_send()
        self.tables[self.q] = self.table[...]
        whole = jnp.zeros((LAYERS + 1, 1, 128), jnp.int32)
        left = whole
        for o in range(ROW):
            value = self.tables[o]
            whole = whole + value
            left = left + jnp.where(o < self.q, value, 0)
        run = whole[LAYERS]
        for z in range(LAYERS):
            self.answer[z] = run + left[z]
            run = run + whole[z]
        for z in range(1, LAYERS):
            self.to_plane(z).start()
        self.sent(True)
        for z in range(1, LAYERS):
            self.to_plane(z).wait_send()

    def result(self):
        self.sent(False)
        self.to_plane(1).wait_recv()


def kernel(
    comm,
    groups,
    ti,
    tc,
    x_hbm,
    wr_hbm,
    sr,
    br,
    ws_hbm,
    ss,
    bs,
    we_hbm,
    se,
    be,
    out,
    x,
    wr,
    ws,
    we,
    xs,
    last,
    acc,
    flat,
    cin,
    spat,
    own,
    spill,
    arrived,
    cnt,
    box,
    table,
    tables,
    answer,
    x_sem,
    wr_sem,
    ws_sem,
    we_sem,
    sems,
    spill_send,
    spill_recv,
):
    channels = x_hbm.shape[2]
    inner = wr_hbm.shape[1]
    chunks = channels // KC

    if comm:
        ex = Exchange(groups, cnt, box, table, tables, answer, sems)
        ex.greet()

    copies_x = []
    copies_r = []
    for k in range(chunks):
        at = pl.ds(k * KC, KC)
        cx = pltpu.make_async_copy(x_hbm.at[:, :, at], x[k], x_sem.at[k])
        cr = pltpu.make_async_copy(wr_hbm.at[at], wr.at[at], wr_sem.at[k])
        cx.start()
        cr.start()
        copies_x.append(cx)
        copies_r.append(cr)
    copies_s = []
    for a in range(3):
        cs = pltpu.make_async_copy(ws_hbm.at[a], ws.at[a], ws_sem.at[a])
        cs.start()
        copies_s.append(cs)
    ce = pltpu.make_async_copy(we_hbm, we, we_sem)
    ce.start()

    count = tc[0]
    if comm:
        cnt[...] = jnp.full((1, 128), count, jnp.int32)

    def moved():
        return pltpu.make_async_remote_copy(
            src_ref=spill,
            dst_ref=arrived,
            send_sem=spill_send,
            recv_sem=spill_recv,
            device_id=ex.ahead,
            device_id_type=MESH,
        )

    def gather(half, k):
        if half == 0:
            slots = [jnp.clip(count - HALF + j, 0, SLOTS - 1) for j in range(HALF)]
        else:
            slots = list(range(HALF))
        at = pl.ds(k * KC, KC)
        for s, slot in enumerate(slots):
            tile = ti[0, slot]
            xs[half, s * BODY : (s + 1) * BODY, at] = x[k][tile, 0:BODY, :]
            last[s : s + 1, at] = x[k][tile, BODY:CELLS, :].astype(f32)
        xs[half, ROWS:FULL, at] = last[:, at].astype(bf16)

    def reduce(half, k):
        at = pl.ds(k * KC, KC)
        part = dot(xs[half, :, at], wr[at, :])
        if k > 0:
            part = part + flat_rows(half)
        if k == chunks - 1:
            part = jnp.maximum(part * sr[...][None, :] + br[...][None, :], 0.0)
        for j in range(inner // LANES):
            flat[half, j] = part[:, j * LANES : (j + 1) * LANES]

    def flat_rows(half):
        return jnp.concatenate([flat[half, j] for j in range(inner // LANES)], axis=1)

    def fold(half):
        none = jnp.zeros((HALF, inner), f32)

        def cell(i, k):
            c = i * SIDE + k
            if i >= SIDE:
                return none
            at = pl.ds(ROWS, HALF) if c == BODY else pl.ds(c, HALF, stride=BODY)
            return jnp.concatenate([flat[half, j, at, :] for j in range(inner // LANES)], axis=1)

        for k in range(SIDE):
            for i in range(FOLD):
                low, high = cell(i, k), cell(i + FOLD, k)
                cin[i + 1, k + 1] = jnp.concatenate([low, high], axis=0).astype(bf16)
                if i == FOLD - 1:
                    cin[0, k + 1] = jnp.concatenate([none, low], axis=0).astype(bf16)
                if i == 0:
                    cin[FOLD + 1, k + 1] = jnp.concatenate([high, none], axis=0).astype(bf16)

    def taps(half, a):
        lhs = jnp.concatenate(
            [
                cin[a : a + FOLD, b : b + SIDE].reshape(FOLD * SIDE * SLOTS, inner)
                for b in range(3)
            ],
            axis=1,
        )
        part = dot(lhs, ws[a].reshape(3 * inner, inner))
        if a > 0:
            part = part + acc[...]
        if a < 2:
            acc[...] = part
            return
        part = jnp.maximum(part * ss[...][None, :] + bs[...][None, :], 0.0)
        for i in range(FOLD):
            for k in range(SIDE):
                for up in range(2):
                    v = (i * SIDE + k) * SLOTS + up * HALF
                    c = (i + up * FOLD) * SIDE + k
                    if c > BODY:
                        continue
                    at = pl.ds(ROWS, HALF) if c == BODY else pl.ds(c, HALF, stride=BODY)
                    for j in range(inner // LANES):
                        flat[half, j, at, :] = part[v : v + HALF, j * LANES : (j + 1) * LANES]
        for j in range(inner // LANES):
            spat[:, j * LANES : (j + 1) * LANES] = flat[half, j].astype(bf16)

    def expand(half):
        for n in range(channels // NC):
            at = pl.ds(n * NC, NC)
            v = dot(spat[...], we[:, at]) * se[at][None, :] + be[at][None, :]
            v = jnp.maximum(v + xs[half, :, at].astype(f32), 0.0)
            v = jnp.sum(v[:ROWS].reshape(HALF, BODY, NC), axis=1) + v[ROWS:FULL]
            v = (v * (1.0 / CELLS)).astype(bf16)
            if half == 0:
                spill[:, at] = v
            else:
                own[:, at] = v

    for i in range(FOLD + 2):
        cin[i, 0] = jnp.zeros((SLOTS, inner), bf16)
        cin[i, SIDE + 1] = jnp.zeros((SLOTS, inner), bf16)
    for k in range(chunks):
        copies_x[k].wait()
        if comm and k == 0:

            @pl.when(ex.z >= LAYERS // 2)
            def _():
                ex.post(False)

        gather(0, k)
        gather(1, k)
        copies_r[k].wait()
        reduce(0, k)
        reduce(1, k)
        if comm and k == 0:

            @pl.when((ex.z > 0) & (ex.z < LAYERS // 2))
            def _():
                ex.post(False)

    fold(0)
    for a in range(3):
        copies_s[a].wait()
        taps(0, a)
    if comm:

        @pl.when(ex.hub)
        def _():
            ex.post(True)

    ce.wait()
    expand(0)
    if comm:
        moved().start()
    fold(1)
    for a in range(3):
        taps(1, a)
    if comm:

        @pl.when(ex.hub)
        def _():
            ex.collect()

    expand(1)

    if comm:

        @pl.when(ex.hub)
        def _():
            ex.settle()

        @pl.when(jnp.logical_not(ex.hub))
        def _():
            ex.result()

        backlog = answer[0] - ex.rank * HALF
        moved().wait()
        prior = arrived[...]
    else:
        backlog = jnp.full((1, 128), 3, jnp.int32)
        prior = spill[...]
    both = jnp.concatenate([prior.astype(f32), own[...].astype(f32)], axis=0).astype(bf16)
    row = lax.broadcasted_iota(jnp.int32, (HALF, SLOTS), 0)
    col = lax.broadcasted_iota(jnp.int32, (HALF, SLOTS), 1)
    pick = jnp.where(col - row == HALF - backlog[:, :SLOTS], 1.0, 0.0).astype(bf16)
    out[...] = dot(pick, both).astype(bf16)


def on_device(comm, groups, tiles, tissue_index, tissue_count, wr, sr, br, ws, ss, bs, we, se, be):
    cand, cells, channels = tiles.shape
    inner = wr.shape[1]
    smem = pl.BlockSpec(memory_space=pltpu.SMEM)
    vmem = pl.BlockSpec(memory_space=pltpu.VMEM)
    hbm = pl.BlockSpec(memory_space=pl.ANY)
    dma = pltpu.SemaphoreType.DMA
    return pl.pallas_call(
        functools.partial(kernel, comm, groups),
        out_shape=jax.ShapeDtypeStruct((HALF, channels), bf16),
        in_specs=[smem, smem, hbm, hbm, vmem, vmem, hbm, vmem, vmem, hbm, vmem, vmem],
        out_specs=vmem,
        scratch_shapes=[
            [pltpu.VMEM((cand, cells, KC), bf16)] * (channels // KC),
            pltpu.VMEM((channels, inner), bf16),
            pltpu.VMEM((3, 3, inner, inner), bf16),
            pltpu.VMEM((inner, channels), bf16),
            pltpu.VMEM((2, FULL, channels), bf16),
            pltpu.VMEM((HALF, channels), f32),
            pltpu.VMEM((FOLD * SIDE * SLOTS, inner), f32),
            pltpu.VMEM((2, inner // LANES, FULL, LANES), f32),
            pltpu.VMEM((FOLD + 2, SIDE + 2, SLOTS, inner), bf16),
            pltpu.VMEM((FULL, inner), bf16),
            pltpu.VMEM((HALF, channels), bf16),
            pltpu.VMEM((HALF, channels), bf16),
            pltpu.VMEM((HALF, channels), bf16),
            pltpu.VMEM((1, 128), jnp.int32),
            pltpu.VMEM((groups * LAYERS, 1, 128), jnp.int32),
            pltpu.VMEM((LAYERS + 1, 1, 128), jnp.int32),
            pltpu.VMEM((ROW, LAYERS + 1, 1, 128), jnp.int32),
            pltpu.VMEM((LAYERS, 1, 128), jnp.int32),
            dma((channels // KC,)),
            dma((channels // KC,)),
            dma((3,)),
            dma,
            [
                dma((groups,)),
                dma,
                dma((ROW - 1,)),
                dma,
                dma((LAYERS - 1,)),
                dma,
            ],
            dma,
            dma,
        ],
        compiler_params=pltpu.CompilerParams(
            collective_id=0 if comm else None,
            has_side_effects=True,
            vmem_limit_bytes=56 * 1024 * 1024,
        ),
        name="bottleneck",
    )(tissue_index, tissue_count, tiles, wr, sr, br, ws, ss, bs, we, se, be)


def solution(mesh):
    axes = ("grp", "ext")
    split = P(axes)
    return jax.shard_map(
        functools.partial(on_device, True, mesh.shape["grp"]),
        mesh=mesh,
        in_specs=(split, split, split) + (P(),) * 9,
        out_specs=split,
        check_vma=False,
    )
```

time: 29.8 us -> 24.3 us (0.82)
  Pallas kernels: 27.6 us -> 22.1 us
    pallas_call x1, Pallas kernels: 27.6 us -> 22.1 us  [on_device(): pl.pallas_call(functools.partial(kernel, comm, groups), out_shape=jax.Sha...]
where the time goes in v3:
time: 24.3 us; the launch traced here: 24.2 us
  Pallas kernels  22.1 us (91%)
  local copies, waits for them, and re-layouts  1.38 us (6%)
  between operations  0.66 us (3%)
    pallas_call x1, Pallas kernels, on_device(): pl.pallas_call(functools.partial(kernel, comm, groups), out_shape=jax.Sha...  22.1 us
    unnamed x1, local copies, waits for them, and re-layouts  1.38 us

profile of v3, /device:TPU:1, one launch (start us, length us, event | category | flops | bytes accessed | tf_op | source)
XLA Modules:
  0.0 24.2 jit_solution(17264681791651017123)
XLA Ops:
  0.7 22.1 %bottleneck.1 = bf16[8,2048]{1,0:T(8,128)(2,1)} custom-call(s32[1,18]{1,0:T(1,128)} %ti.1, s32[1]{0:T(128)S(6)} %copy.14.tc, bf16[18,49,2048]{2,1,0:T(8,128)(2,1)} %x_hbm.1, bf16[2048,512]{1,0:T(8,128)(2,1)} %wr_hbm.1, f32[512]{0:T(512)} %sr.1, f32[512]{0:T(512)} %br.1, bf16[3,3,512,512]{3,2,1,0:T(8,128)(2,1)} %ws_hbm.1, f32[512]{0:T(512)} %ss.1, f32[512]{0:T(512)} %bs.1, ...), custom_call_target="tpu_custom_call" | custom-call | tf_op jit(solution)/shard_map/bottleneck/pallas_call | solution.py:407
  22.8 1.4 %copy.15 = bf16[8,2048]{1,0:T(8,128)(2,1)} copy(bf16[8,2048]{1,0:T(8,128)(2,1)} %bottleneck.1) | data formatting | bytes 65536

commit v4 on v3

--- a/solution.py
+++ b/solution.py
@@ -16,9 +16,10 @@
 ROWS = HALF * BODY
 FULL = ROWS + HALF
 FOLD = 4
-KC = 1024
+KC = 512
 NC = 256
 LAYERS = 8
+AHEAD = 4
 ROW = 8
 LANES = 128
 bf16 = jnp.bfloat16
@@ -103,15 +104,17 @@
     def collect(self):
         self.all_of(self.box, self.post_recv)
         self.box[self.g * LAYERS] = self.cnt[...]
+        lane = lax.broadcasted_iota(jnp.int32, (1, 128), 1)
         lower = jnp.zeros((1, 128), jnp.int32)
         for y in range(self.groups):
             plane = self.box[y * LAYERS]
             for z in range(1, LAYERS):
                 plane = plane + self.box[y * LAYERS + z]
             lower = lower + jnp.where(y < self.g, plane, 0)
+        table = jnp.where(lane == LAYERS, lower, 0)
         for z in range(LAYERS):
-            self.table[z] = self.box[self.g * LAYERS + z]
-        self.table[LAYERS] = lower
+            table = jnp.where(lane == z, self.box[self.g * LAYERS + z], table)
+        self.table[...] = table
         for k, o in enumerate(self.mates):
             self.to_mate(k, o).start()
 
@@ -127,8 +130,8 @@
 
     def to_plane(self, z):
         return pltpu.make_async_remote_copy(
-            src_ref=self.answer.at[z],
-            dst_ref=self.answer.at[0],
+            src_ref=self.answer,
+            dst_ref=self.answer,
             send_sem=self.out_send.at[z - 1],
             recv_sem=self.out_recv,
             device_id=(self.g, z * ROW + self.q),
@@ -137,46 +140,53 @@
 
     def settle(self):
         self.all_of(self.tables, self.row_recv)
-        for k, o in enumerate(self.mates):
-            self.to_mate(k, o).wait_send()
-        self.tables[self.q] = self.table[...]
-        whole = jnp.zeros((LAYERS + 1, 1, 128), jnp.int32)
-        left = whole
+        mine = self.table[...]
+        whole = mine
+        left = jnp.zeros((1, 128), jnp.int32)
         for o in range(ROW):
-            value = self.tables[o]
+            value = jnp.where(o == self.q, 0, self.tables[o])
             whole = whole + value
             left = left + jnp.where(o < self.q, value, 0)
-        run = whole[LAYERS]
-        for z in range(LAYERS):
-            self.answer[z] = run + left[z]
-            run = run + whole[z]
+        self.answer[0] = whole
+        self.answer[1] = left
         for z in range(1, LAYERS):
             self.to_plane(z).start()
-        self.sent(True)
-        for z in range(1, LAYERS):
-            self.to_plane(z).wait_send()
 
     def result(self):
-        self.sent(False)
         self.to_plane(1).wait_recv()
+
+    def offset(self):
+        lane = lax.broadcasted_iota(jnp.int32, (1, 128), 1)
+        take = jnp.where((lane < self.z) | (lane == LAYERS), self.answer[0], 0)
+        take = take + jnp.where(lane == self.z, self.answer[1], 0)
+        return jnp.sum(take, axis=1, keepdims=True)
+
+    def close(self, hub):
+        self.sent(hub)
+        if hub:
+            for k, o in enumerate(self.mates):
+                self.to_mate(k, o).wait_send()
+            for z in range(1, LAYERS):
+                self.to_plane(z).wait_send()
 
 
 def kernel(
     comm,
     groups,
-    ti,
-    tc,
+    ti_hbm,
+    tc_hbm,
     x_hbm,
     wr_hbm,
-    sr,
-    br,
+    sr_hbm,
+    br_hbm,
     ws_hbm,
-    ss,
-    bs,
+    ss_hbm,
+    bs_hbm,
     we_hbm,
-    se,
-    be,
+    se_hbm,
+    be_hbm,
     out,
+    small,
     x,
     wr,
     ws,
@@ -195,6 +205,7 @@
     table,
     tables,
     answer,
+    small_sem,
     x_sem,
     wr_sem,
     ws_sem,
@@ -209,25 +220,47 @@
 
     if comm:
         ex = Exchange(groups, cnt, box, table, tables, answer, sems)
-        ex.greet()
-
-    copies_x = []
-    copies_r = []
+
+    ti, tc, sr, br, ss, bs, se, be = small
+    fetched = [
+        pltpu.make_async_copy(a, b, small_sem.at[n])
+        for n, (a, b) in enumerate(
+            zip((ti_hbm, tc_hbm, sr_hbm, br_hbm, ss_hbm, bs_hbm, se_hbm, be_hbm), small)
+        )
+    ]
+    units = []
     for k in range(chunks):
         at = pl.ds(k * KC, KC)
-        cx = pltpu.make_async_copy(x_hbm.at[:, :, at], x[k], x_sem.at[k])
-        cr = pltpu.make_async_copy(wr_hbm.at[at], wr.at[at], wr_sem.at[k])
-        cx.start()
-        cr.start()
-        copies_x.append(cx)
-        copies_r.append(cr)
-    copies_s = []
+        units.append(
+            [
+                pltpu.make_async_copy(x_hbm.at[:, :, at], x[k], x_sem.at[k]),
+                pltpu.make_async_copy(wr_hbm.at[at], wr.at[at], wr_sem.at[k]),
+            ]
+        )
     for a in range(3):
-        cs = pltpu.make_async_copy(ws_hbm.at[a], ws.at[a], ws_sem.at[a])
-        cs.start()
-        copies_s.append(cs)
-    ce = pltpu.make_async_copy(we_hbm, we, we_sem)
-    ce.start()
+        units.append([pltpu.make_async_copy(ws_hbm.at[a], ws.at[a], ws_sem.at[a])])
+    units.append([pltpu.make_async_copy(we_hbm, we, we_sem)])
+
+    def begin(n):
+        if n < len(units):
+            for c in units[n]:
+                c.start()
+
+    def ready(n):
+        for c in units[n]:
+            c.wait()
+        begin(n + AHEAD)
+
+    for c in fetched[:2]:
+        c.start()
+    for n in range(AHEAD):
+        begin(n)
+    for c in fetched[2:]:
+        c.start()
+    if comm:
+        ex.greet()
+    for c in fetched[:2]:
+        c.wait()
 
     count = tc[0]
     if comm:
@@ -330,17 +363,19 @@
     for i in range(FOLD + 2):
         cin[i, 0] = jnp.zeros((SLOTS, inner), bf16)
         cin[i, SIDE + 1] = jnp.zeros((SLOTS, inner), bf16)
+    if comm:
+
+        @pl.when(ex.z >= LAYERS // 2)
+        def _():
+            ex.post(False)
+
     for k in range(chunks):
-        copies_x[k].wait()
-        if comm and k == 0:
-
-            @pl.when(ex.z >= LAYERS // 2)
-            def _():
-                ex.post(False)
-
+        ready(k)
         gather(0, k)
         gather(1, k)
-        copies_r[k].wait()
+        if k == chunks - 1:
+            for c in fetched[2:]:
+                c.wait()
         reduce(0, k)
         reduce(1, k)
         if comm and k == 0:
@@ -351,7 +386,7 @@
 
     fold(0)
     for a in range(3):
-        copies_s[a].wait()
+        ready(chunks + a)
         taps(0, a)
     if comm:
 
@@ -359,57 +394,67 @@
         def _():
             ex.post(True)
 
-    ce.wait()
+    ready(chunks + 3)
     expand(0)
     if comm:
         moved().start()
     fold(1)
     for a in range(3):
         taps(1, a)
+    expand(1)
+
     if comm:
 
         @pl.when(ex.hub)
         def _():
             ex.collect()
-
-    expand(1)
-
-    if comm:
-
-        @pl.when(ex.hub)
-        def _():
             ex.settle()
 
         @pl.when(jnp.logical_not(ex.hub))
         def _():
             ex.result()
 
-        backlog = answer[0] - ex.rank * HALF
-        moved().wait()
+        backlog = ex.offset() - ex.rank * HALF
+        moved().wait_recv()
         prior = arrived[...]
     else:
-        backlog = jnp.full((1, 128), 3, jnp.int32)
+        backlog = jnp.full((1, 1), 3, jnp.int32)
         prior = spill[...]
     both = jnp.concatenate([prior.astype(f32), own[...].astype(f32)], axis=0).astype(bf16)
     row = lax.broadcasted_iota(jnp.int32, (HALF, SLOTS), 0)
     col = lax.broadcasted_iota(jnp.int32, (HALF, SLOTS), 1)
-    pick = jnp.where(col - row == HALF - backlog[:, :SLOTS], 1.0, 0.0).astype(bf16)
+    pick = jnp.where(col - row == HALF - backlog, 1.0, 0.0).astype(bf16)
     out[...] = dot(pick, both).astype(bf16)
+    if comm:
+        moved().wait_send()
+
+        @pl.when(ex.hub)
+        def _():
+            ex.close(True)
+
+        @pl.when(jnp.logical_not(ex.hub))
+        def _():
+            ex.close(False)
 
 
 def on_device(comm, groups, tiles, tissue_index, tissue_count, wr, sr, br, ws, ss, bs, we, se, be):
     cand, cells, channels = tiles.shape
     inner = wr.shape[1]
-    smem = pl.BlockSpec(memory_space=pltpu.SMEM)
     vmem = pl.BlockSpec(memory_space=pltpu.VMEM)
     hbm = pl.BlockSpec(memory_space=pl.ANY)
     dma = pltpu.SemaphoreType.DMA
     return pl.pallas_call(
         functools.partial(kernel, comm, groups),
         out_shape=jax.ShapeDtypeStruct((HALF, channels), bf16),
-        in_specs=[smem, smem, hbm, hbm, vmem, vmem, hbm, vmem, vmem, hbm, vmem, vmem],
+        in_specs=[hbm] * 12,
         out_specs=vmem,
         scratch_shapes=[
+            [
+                pltpu.SMEM((1, cand), jnp.int32),
+                pltpu.SMEM((1,), jnp.int32),
+            ]
+            + [pltpu.VMEM((inner,), f32)] * 4
+            + [pltpu.VMEM((channels,), f32)] * 2,
             [pltpu.VMEM((cand, cells, KC), bf16)] * (channels // KC),
             pltpu.VMEM((channels, inner), bf16),
             pltpu.VMEM((3, 3, inner, inner), bf16),
@@ -425,9 +470,10 @@
             pltpu.VMEM((HALF, channels), bf16),
             pltpu.VMEM((1, 128), jnp.int32),
             pltpu.VMEM((groups * LAYERS, 1, 128), jnp.int32),
-            pltpu.VMEM((LAYERS + 1, 1, 128), jnp.int32),
-            pltpu.VMEM((ROW, LAYERS + 1, 1, 128), jnp.int32),
-            pltpu.VMEM((LAYERS, 1, 128), jnp.int32),
+            pltpu.VMEM((1, 128), jnp.int32),
+            pltpu.VMEM((ROW, 1, 128), jnp.int32),
+            pltpu.VMEM((2, 1, 128), jnp.int32),
+            dma((8,)),
             dma((channels // KC,)),
             dma((channels // KC,)),
             dma((3,)),

time: 24.3 us -> 22.3 us (0.918); the launches traced: 24.2 us -> 21.9 us
  Pallas kernels: 22.1 us -> 19.8 us
    pallas_call x1, Pallas kernels: 22.1 us -> 19.8 us  [on_device(): pl.pallas_call(functools.partial(kernel, comm, groups), out_shape=jax.Sha...]
where the time goes in v4:
time: 22.3 us; the launch traced here: 21.9 us
  Pallas kernels  19.8 us (89%)
  local copies, waits for them, and re-layouts  1.38 us (6%)
  between operations  0.66 us (3%)
    pallas_call x1, Pallas kernels, on_device(): pl.pallas_call(functools.partial(kernel, comm, groups), out_shape=jax.Sha...  19.8 us
    unnamed x1, local copies, waits for them, and re-layouts  1.38 us

profile of v4, /device:TPU:1, one launch (start us, length us, event | category | flops | bytes accessed | tf_op | source)
XLA Modules:
  0.0 21.9 jit_solution(10136601634107861640)
XLA Ops:
  0.7 19.8 %bottleneck.1 = bf16[8,2048]{1,0:T(8,128)(2,1)} custom-call(s32[1,18]{1,0:T(1,128)} %ti_hbm.1, s32[1]{0:T(128)S(6)} %copy.14.tc_hbm, bf16[18,49,2048]{2,1,0:T(8,128)(2,1)} %x_hbm.1, bf16[2048,512]{1,0:T(8,128)(2,1)} %wr_hbm.1, f32[512]{0:T(512)} %sr_hbm.1, f32[512]{0:T(512)} %br_hbm.1, bf16[3,3,512,512]{3,2,1,0:T(8,128)(2,1)} %ws_hbm.1, f32[512]{0:T(512)} %ss_hbm.1, ...), custom_call_target="tpu_custom_call" | custom-call | tf_op jit(solution)/shard_map/bottleneck/pallas_call | solution.py:446
  20.5 1.4 %copy.15 = bf16[8,2048]{1,0:T(8,128)(2,1)} copy(bf16[8,2048]{1,0:T(8,128)(2,1)} %bottleneck.1) | data formatting | bytes 65536

commit v5 on v4

--- a/solution.py
+++ b/solution.py
@@ -41,13 +41,12 @@
         self.z = e // ROW
         self.q = lax.rem(e, ROW)
         self.rank = g * ext + e
-        total = groups * ext
+        total = self.total = groups * ext
         self.hub = self.z == 0
         after = lax.rem(self.rank + 1, total)
         before = lax.rem(self.rank + total - 1, total)
         self.ahead = (after // ext, lax.rem(after, ext))
         self.behind = (before // ext, lax.rem(before, ext))
-        self.far = [lax.rem(g + k, groups) for k in range(groups)]
         self.mates = [lax.rem(self.q + k, ROW) for k in range(1, ROW)]
 
     def greet(self):
@@ -58,10 +57,17 @@
 
         @pl.when(self.hub)
         def _():
-            for z in reversed(range(LAYERS)):
-                for k, y in enumerate(self.far):
-                    if z > 0 or k > 0:
+            for y in reversed(range(self.groups)):
+
+                @pl.when(y < self.g)
+                def _():
+                    tell((y, self.q))
+
+                @pl.when(y <= self.g)
+                def _():
+                    for z in reversed(range(1, LAYERS)):
                         tell((y, z * ROW + self.q))
+
             for o in self.mates:
                 tell((self.g, o))
 
@@ -71,42 +77,46 @@
 
         tell(self.behind)
 
-    def to_hub(self, k, y):
-        mine = self.g * LAYERS + self.z
+    def to_hub(self, y):
         return pltpu.make_async_remote_copy(
             src_ref=self.cnt,
-            dst_ref=self.box.at[mine],
-            send_sem=self.post_send.at[k],
+            dst_ref=self.box.at[self.g * LAYERS + self.z],
+            send_sem=self.post_send.at[y],
             recv_sem=self.post_recv,
             device_id=(y, self.q),
             device_id_type=MESH,
         )
 
+    def each_hub(self, hub, act):
+        for y in range(self.groups):
+
+            @pl.when(y > self.g if hub else y >= self.g)
+            def _():
+                act(self.to_hub(y))
+
     def post(self, hub):
-        barrier = pltpu.get_barrier_semaphore()
-        if hub:
-            pl.semaphore_wait(barrier, self.groups - 1 + ROW - 1 + LAYERS - 1 + 1)
-        else:
-            pl.semaphore_wait(barrier, self.groups + 1)
-        for k, y in enumerate(self.far):
-            if not hub or k > 0:
-                self.to_hub(k, y).start()
+        own = ROW - 1 + LAYERS - 1 if hub else 1
+        pl.semaphore_wait(pltpu.get_barrier_semaphore(), self.groups - 1 - self.g + own + 1)
+        self.each_hub(hub, lambda c: c.start())
 
     def sent(self, hub):
-        for k, y in enumerate(self.far):
-            if not hub or k > 0:
-                self.to_hub(k, y).wait_send()
-
-    def all_of(self, box, sem):
-        rows = box.at[pl.ds(0, box.shape[0] - 1)]
+        self.each_hub(hub, lambda c: c.wait_send())
+
+    def all_of(self, box, count, sem):
+        rows = box.at[pl.ds(0, count - 1)]
         pltpu.make_async_copy(rows, rows, sem).wait()
 
     def collect(self):
-        self.all_of(self.box, self.post_recv)
+        for y in range(self.groups):
+
+            @pl.when(y == self.g)
+            def _():
+                self.all_of(self.box, (y + 1) * LAYERS, self.post_recv)
+
         self.box[self.g * LAYERS] = self.cnt[...]
         lane = lax.broadcasted_iota(jnp.int32, (1, 128), 1)
         lower = jnp.zeros((1, 128), jnp.int32)
-        for y in range(self.groups):
+        for y in range(self.groups - 1):
             plane = self.box[y * LAYERS]
             for z in range(1, LAYERS):
                 plane = plane + self.box[y * LAYERS + z]
@@ -139,7 +149,7 @@
         )
 
     def settle(self):
-        self.all_of(self.tables, self.row_recv)
+        self.all_of(self.tables, ROW, self.row_recv)
         mine = self.table[...]
         whole = mine
         left = jnp.zeros((1, 128), jnp.int32)
@@ -397,17 +407,26 @@
     ready(chunks + 3)
     expand(0)
     if comm:
-        moved().start()
+
+        @pl.when(ex.rank < ex.total - 1)
+        def _():
+            moved().start()
+
     fold(1)
     for a in range(3):
         taps(1, a)
+        if comm and a == 1:
+
+            @pl.when(ex.hub)
+            def _():
+                ex.collect()
+
     expand(1)
 
     if comm:
 
         @pl.when(ex.hub)
         def _():
-            ex.collect()
             ex.settle()
 
         @pl.when(jnp.logical_not(ex.hub))
@@ -415,7 +434,15 @@
             ex.result()
 
         backlog = ex.offset() - ex.rank * HALF
-        moved().wait_recv()
+
+        @pl.when(ex.rank > 0)
+        def _():
+            moved().wait_recv()
+
+        @pl.when(ex.rank == 0)
+        def _():
+            arrived[...] = own[...]
+
         prior = arrived[...]
     else:
         backlog = jnp.full((1, 1), 3, jnp.int32)
@@ -426,7 +453,11 @@
     pick = jnp.where(col - row == HALF - backlog, 1.0, 0.0).astype(bf16)
     out[...] = dot(pick, both).astype(bf16)
     if comm:
-        moved().wait_send()
+
+        @pl.when(ex.rank < ex.total - 1)
+        def _():
+            moved().wait_send()
+
 
         @pl.when(ex.hub)
         def _():
@@ -445,7 +476,7 @@
     dma = pltpu.SemaphoreType.DMA
     return pl.pallas_call(
         functools.partial(kernel, comm, groups),
-        out_shape=jax.ShapeDtypeStruct((HALF, channels), bf16),
+        out_shape=pltpu.VMEM((HALF, channels), bf16),
         in_specs=[hbm] * 12,
         out_specs=vmem,
         scratch_shapes=[

time: 22.3 us -> 19.6 us (0.88)
  the two profiles are of different devices: /device:TPU:1 before, /device:TPU:24 now
where the time goes in v5:
time: 19.6 us; the launch traced here: 19.5 us
  Pallas kernels  18.2 us (93%)
  between operations  0.66 us (3%)
  local copies, waits for them, and re-layouts  0.62 us (3%)
    pallas_call x1, Pallas kernels, on_device(): pl.pallas_call(functools.partial(kernel, comm, groups), out_shape=pltpu.V...  18.2 us
    unnamed x1, local copies, waits for them, and re-layouts  0.62 us

profile of v5, /device:TPU:24, one launch (start us, length us, event | category | flops | bytes accessed | tf_op | source)
XLA Modules:
  0.0 19.5 jit_solution(9657172750502676984)
XLA Ops:
  0.7 18.2 %bottleneck.1 = bf16[8,2048]{1,0:T(8,128)(2,1)S(1)} custom-call(s32[1,18]{1,0:T(1,128)} %ti_hbm.1, s32[1]{0:T(128)S(6)} %copy.15.tc_hbm, bf16[18,49,2048]{2,1,0:T(8,128)(2,1)} %x_hbm.1, bf16[2048,512]{1,0:T(8,128)(2,1)} %wr_hbm.1, f32[512]{0:T(512)} %sr_hbm.1, f32[512]{0:T(512)} %br_hbm.1, bf16[3,3,512,512]{3,2,1,0:T(8,128)(2,1)} %ws_hbm.1, f32[512]{0:T(512)} %ss_hbm.1, ...), custom_call_target="tpu_custom_call" | custom-call | tf_op jit(solution)/shard_map/bottleneck/pallas_call | solution.py:477
  18.9 0.6 %copy.14 = bf16[8,2048]{1,0:T(8,128)(2,1)} copy(bf16[8,2048]{1,0:T(8,128)(2,1)S(1)} %bottleneck.1) | data formatting | bytes 65536

commit v6 on v5

--- a/solution.py
+++ b/solution.py
@@ -434,6 +434,13 @@
             ex.result()
 
         backlog = ex.offset() - ex.rank * HALF
+    else:
+        backlog = jnp.full((1, 1), 3, jnp.int32)
+    row = lax.broadcasted_iota(jnp.int32, (HALF, HALF), 0)
+    col = lax.broadcasted_iota(jnp.int32, (HALF, HALF), 1)
+    stay = dot(jnp.where(col - row == -backlog, 1.0, 0.0), own[...].astype(f32))
+    come = jnp.where(col - row == HALF - backlog, 1.0, 0.0)
+    if comm:
 
         @pl.when(ex.rank > 0)
         def _():
@@ -445,13 +452,8 @@
 
         prior = arrived[...]
     else:
-        backlog = jnp.full((1, 1), 3, jnp.int32)
         prior = spill[...]
-    both = jnp.concatenate([prior.astype(f32), own[...].astype(f32)], axis=0).astype(bf16)
-    row = lax.broadcasted_iota(jnp.int32, (HALF, SLOTS), 0)
-    col = lax.broadcasted_iota(jnp.int32, (HALF, SLOTS), 1)
-    pick = jnp.where(col - row == HALF - backlog, 1.0, 0.0).astype(bf16)
-    out[...] = dot(pick, both).astype(bf16)
+    out[...] = (stay + dot(come, prior.astype(f32))).astype(bf16)
     if comm:
 
         @pl.when(ex.rank < ex.total - 1)

time: 19.6 us -> 19.6 us (level)
  no operation moved by 1% of the time
where the time goes in v6:
time: 19.6 us; the launch traced here: 19.5 us
  Pallas kernels  18.2 us (93%)
  between operations  0.66 us (3%)
  local copies, waits for them, and re-layouts  0.62 us (3%)
    pallas_call x1, Pallas kernels, on_device(): pl.pallas_call(functools.partial(kernel, comm, groups), out_shape=pltpu.V...  18.2 us
    unnamed x1, local copies, waits for them, and re-layouts  0.62 us

profile of v6, /device:TPU:24, one launch (start us, length us, event | category | flops | bytes accessed | tf_op | source)
XLA Modules:
  0.0 19.5 jit_solution(14782626527599078134)
XLA Ops:
  0.7 18.2 %bottleneck.1 = bf16[8,2048]{1,0:T(8,128)(2,1)S(1)} custom-call(s32[1,18]{1,0:T(1,128)} %ti_hbm.1, s32[1]{0:T(128)S(6)} %copy.15.tc_hbm, bf16[18,49,2048]{2,1,0:T(8,128)(2,1)} %x_hbm.1, bf16[2048,512]{1,0:T(8,128)(2,1)} %wr_hbm.1, f32[512]{0:T(512)} %sr_hbm.1, f32[512]{0:T(512)} %br_hbm.1, bf16[3,3,512,512]{3,2,1,0:T(8,128)(2,1)} %ws_hbm.1, f32[512]{0:T(512)} %ss_hbm.1, ...), custom_call_target="tpu_custom_call" | custom-call | tf_op jit(solution)/shard_map/bottleneck/pallas_call | solution.py:479
  18.9 0.6 %copy.14 = bf16[8,2048]{1,0:T(8,128)(2,1)} copy(bf16[8,2048]{1,0:T(8,128)(2,1)S(1)} %bottleneck.1) | data formatting | bytes 65536

commit v7 on v5

--- a/solution.py
+++ b/solution.py
@@ -276,12 +276,12 @@
     if comm:
         cnt[...] = jnp.full((1, 128), count, jnp.int32)
 
-    def moved():
+    def moved(h):
         return pltpu.make_async_remote_copy(
-            src_ref=spill,
-            dst_ref=arrived,
-            send_sem=spill_send,
-            recv_sem=spill_recv,
+            src_ref=spill[h],
+            dst_ref=arrived[h],
+            send_sem=spill_send.at[h],
+            recv_sem=spill_recv.at[h],
             device_id=ex.ahead,
             device_id_type=MESH,
         )
@@ -358,6 +358,11 @@
         for j in range(inner // LANES):
             spat[:, j * LANES : (j + 1) * LANES] = flat[half, j].astype(bf16)
 
+    def send_spill(h):
+        @pl.when(ex.rank < ex.total - 1)
+        def _():
+            moved(h).start()
+
     def expand(half):
         for n in range(channels // NC):
             at = pl.ds(n * NC, NC)
@@ -366,7 +371,10 @@
             v = jnp.sum(v[:ROWS].reshape(HALF, BODY, NC), axis=1) + v[ROWS:FULL]
             v = (v * (1.0 / CELLS)).astype(bf16)
             if half == 0:
-                spill[:, at] = v
+                per = channels // NC // 2
+                spill[n // per][:, n % per * NC : (n % per + 1) * NC] = v
+                if comm and n % per == per - 1:
+                    send_spill(n // per)
             else:
                 own[:, at] = v
 
@@ -406,12 +414,6 @@
 
     ready(chunks + 3)
     expand(0)
-    if comm:
-
-        @pl.when(ex.rank < ex.total - 1)
-        def _():
-            moved().start()
-
     fold(1)
     for a in range(3):
         taps(1, a)
@@ -437,16 +439,18 @@
 
         @pl.when(ex.rank > 0)
         def _():
-            moved().wait_recv()
+            for h in range(2):
+                moved(h).wait_recv()
 
         @pl.when(ex.rank == 0)
         def _():
-            arrived[...] = own[...]
-
-        prior = arrived[...]
+            for h in range(2):
+                arrived[h][...] = jnp.zeros_like(arrived[h])
+
+        prior = jnp.concatenate([arrived[h][...] for h in range(2)], axis=1)
     else:
         backlog = jnp.full((1, 1), 3, jnp.int32)
-        prior = spill[...]
+        prior = jnp.concatenate([spill[h][...] for h in range(2)], axis=1)
     both = jnp.concatenate([prior.astype(f32), own[...].astype(f32)], axis=0).astype(bf16)
     row = lax.broadcasted_iota(jnp.int32, (HALF, SLOTS), 0)
     col = lax.broadcasted_iota(jnp.int32, (HALF, SLOTS), 1)
@@ -456,7 +460,8 @@
 
         @pl.when(ex.rank < ex.total - 1)
         def _():
-            moved().wait_send()
+            for h in range(2):
+                moved(h).wait_send()
 
 
         @pl.when(ex.hub)
@@ -497,8 +502,8 @@
             pltpu.VMEM((FOLD + 2, SIDE + 2, SLOTS, inner), bf16),
             pltpu.VMEM((FULL, inner), bf16),
             pltpu.VMEM((HALF, channels), bf16),
-            pltpu.VMEM((HALF, channels), bf16),
-            pltpu.VMEM((HALF, channels), bf16),
+            [pltpu.VMEM((HALF, channels // 2), bf16)] * 2,
+            [pltpu.VMEM((HALF, channels // 2), bf16)] * 2,
             pltpu.VMEM((1, 128), jnp.int32),
             pltpu.VMEM((groups * LAYERS, 1, 128), jnp.int32),
             pltpu.VMEM((1, 128), jnp.int32),
@@ -517,8 +522,8 @@
                 dma((LAYERS - 1,)),
                 dma,
             ],
-            dma,
-            dma,
+            dma((2,)),
+            dma((2,)),
         ],
         compiler_params=pltpu.CompilerParams(
             collective_id=0 if comm else None,

time: 19.6 us -> 19.5 us (level)
  no operation moved by 1% of the time
where the time goes in v7:
time: 19.5 us
  Pallas kernels  18.2 us (93%)
  between operations  0.66 us (3%)
  local copies, waits for them, and re-layouts  0.62 us (3%)
    pallas_call x1, Pallas kernels, on_device(): pl.pallas_call(functools.partial(kernel, comm, groups), out_shape=pltpu.V...  18.2 us
    unnamed x1, local copies, waits for them, and re-layouts  0.62 us

profile of v7, /device:TPU:24, one launch (start us, length us, event | category | flops | bytes accessed | tf_op | source)
XLA Modules:
  0.0 19.5 jit_solution(734378511781265692)
XLA Ops:
  0.7 18.2 %bottleneck.1 = bf16[8,2048]{1,0:T(8,128)(2,1)S(1)} custom-call(s32[1,18]{1,0:T(1,128)} %ti_hbm.1, s32[1]{0:T(128)S(6)} %copy.15.tc_hbm, bf16[18,49,2048]{2,1,0:T(8,128)(2,1)} %x_hbm.1, bf16[2048,512]{1,0:T(8,128)(2,1)} %wr_hbm.1, f32[512]{0:T(512)} %sr_hbm.1, f32[512]{0:T(512)} %br_hbm.1, bf16[3,3,512,512]{3,2,1,0:T(8,128)(2,1)} %ws_hbm.1, f32[512]{0:T(512)} %ss_hbm.1, ...), custom_call_target="tpu_custom_call" | custom-call | tf_op jit(solution)/shard_map/bottleneck/pallas_call | solution.py:482
  18.8 0.6 %copy.14 = bf16[8,2048]{1,0:T(8,128)(2,1)} copy(bf16[8,2048]{1,0:T(8,128)(2,1)S(1)} %bottleneck.1) | data formatting | bytes 65536
